TPU v7x, 512 devices: a whole 4x4x16 slice. The times are simulated.
512 devices in a mesh: query: 2 (over core), key: 8 (over x, y_hi), heads: 32 (over z, y_lo).
Axes of the slice: x: 4, y: 4 (y_hi: 2, y_lo: 2; y = y_hi * 2 + y_lo), z: 16, core: 2. Of those that a mesh axis runs over, the one named last changes fastest.
Arguments:
- pair_feats: bfloat16 [1024, 64, 8192], P(('query', 'heads'), None, 'key'), may hold values from -6 to 6
- bucket_ids: int32 [1024, 8192], P(('query', 'heads'), 'key'), may hold values from 0 to 31
- ln_gain: float32 [64], replicated, may hold values from 0.5 to 1.5
- w_in: bfloat16 [64, 256], replicated, may hold values from -0.75 to 0.75
- b_in: float32 [256], replicated, may hold values from -3 to 3
- w_out: bfloat16 [256, 32], replicated, may hold values from -0.375 to 0.375
- bucket_table: bfloat16 [32, 32], replicated, may hold values from -4 to 4
- key_mask: int32 [8192], P('key'), may hold values 0 or 1
- q_heads: bfloat16 [32, 32, 1024], P('heads', None, 'query'), may hold values from -6 to 6
- k_heads: bfloat16 [32, 32, 8192], P('heads', None, 'key'), may hold values from -6 to 6
- v_heads: bfloat16 [32, 32, 8192], P('heads', None, 'key'), may hold values from -6 to 6
- out_heads: bfloat16 [32, 32, 1024], P('heads', None, 'query'), may hold values from -6 to 6
- dout_heads: bfloat16 [32, 32, 1024], P('heads', None, 'query'), may hold values from -96 to 96
- log_norm: float32 [32, 1024], P('heads', 'query'), may hold values from 8 to 10
Outputs:
- grad_pairs: bfloat16 [1024, 64, 8192], P(('query', 'heads'), None, 'key')
- grad_q: bfloat16 [32, 32, 1024], P('heads', None, 'query')
- grad_k: bfloat16 [32, 32, 8192], P('heads', None, 'key')
- grad_v: bfloat16 [32, 32, 8192], P('heads', None, 'key')
All inputs are finite; a program needn't handle non-finite values. No bound on the sum of `key_mask` on one device may be relied on, other than what follows from the above.
Results may differ from a plain program's by a relative error of at most 0.012.
The roundings to bfloat16 on the way count: a program that leaves them out, or rounds other values in their place, can miss the bound.
Values may be sent and summed in bfloat16 or wider, within the bound.
A program may use at most 64 MiB of HBM per device.

v0:
```python
import math

import jax
import jax.numpy as jnp
from jax import lax
from jax.sharding import PartitionSpec as P


def gelu_parts(pre_act):
    cdf_val = 0.5 * (1.0 + jax.scipy.special.erf(pre_act * (1.0 / math.sqrt(2.0))))
    density = jnp.exp(-0.5 * pre_act * pre_act) * (1.0 / math.sqrt(2.0 * math.pi))
    return (pre_act * cdf_val, cdf_val + pre_act * density)


def normalize(pair_blk, ln_gain):
    values = pair_blk.astype(jnp.float32)
    centre = values - jnp.mean(values, axis=1, keepdims=True)
    inv_std = lax.rsqrt(jnp.mean(centre * centre, axis=1, keepdims=True) + 1e-05)
    unit_pairs = centre * inv_std
    normed = (unit_pairs * ln_gain[None, :, None]).astype(jnp.bfloat16)
    return (unit_pairs, inv_std, normed)


def by_groups(kernel_fn, arrays, group_rows):
    stacked = tuple(
        (
            member.reshape((member.shape[0] // group_rows, group_rows) + member.shape[1:])
            for member in arrays
        )
    )
    result = lax.map(lambda blocks: kernel_fn(*blocks), stacked)
    return jax.tree.map(
        lambda member: member.reshape((member.shape[0] * group_rows,) + member.shape[2:]), result
    )


def per_device(
    pair_feats,
    bucket_ids,
    ln_gain,
    w_in,
    b_in,
    w_out,
    bucket_table,
    key_mask,
    q_heads,
    k_heads,
    v_heads,
    out_heads,
    dout_heads,
    log_norm,
):
    pair_rows = pair_feats.shape[0]
    score_scale = 1.0 / math.sqrt(q_heads.shape[1])
    group_rows = math.gcd(pair_rows, 4)
    num_buckets = bucket_table.shape[0]
    deltas = jnp.sum(dout_heads.astype(jnp.float32) * out_heads.astype(jnp.float32), axis=1)
    delta_cols = jnp.transpose(deltas)[:, :, None]
    norm_cols = jnp.transpose(log_norm)[:, :, None]

    def forward_rows(pair_blk, bucket_blk):
        unit_pairs, inv_std, normed = normalize(pair_blk, ln_gain)
        pre_act = (
            jnp.einsum("rck,cf->rfk", normed, w_in, preferred_element_type=jnp.float32)
            + b_in[None, :, None]
        )
        gelu_val, gelu_slope = gelu_parts(pre_act)
        hidden = gelu_val.astype(jnp.bfloat16)
        bucket_iota = lax.broadcasted_iota(jnp.int32, (1, num_buckets, 1), 1)
        onehot = (bucket_blk[:, None, :] == bucket_iota).astype(jnp.bfloat16)
        lookup = jnp.einsum("rbk,bh->rhk", onehot, bucket_table, preferred_element_type=jnp.float32)
        mixed = jnp.einsum("rfk,fh->rhk", hidden, w_out, preferred_element_type=jnp.float32)
        return ((mixed + lookup).astype(jnp.bfloat16), unit_pairs, inv_std, normed)

    def backward_rows(unit_pairs, inv_std, normed, grad_blk):
        pre_act = (
            jnp.einsum("rck,cf->rfk", normed, w_in, preferred_element_type=jnp.float32)
            + b_in[None, :, None]
        )
        gelu_val, gelu_slope = gelu_parts(pre_act)
        dhidden = jnp.einsum("rhk,fh->rfk", grad_blk, w_out, preferred_element_type=jnp.float32)
        dpre = (dhidden * gelu_slope).astype(jnp.bfloat16)
        dunit = (
            jnp.einsum("rfk,cf->rck", dpre, w_in, preferred_element_type=jnp.float32)
            * ln_gain[None, :, None]
        )
        first_mean = jnp.mean(dunit, axis=1, keepdims=True)
        second_mean = jnp.mean(dunit * unit_pairs, axis=1, keepdims=True)
        return (inv_std * (dunit - first_mean - unit_pairs * second_mean)).astype(jnp.bfloat16)

    pair_blk = pair_feats
    bucket_blk = bucket_ids
    bias_vals, unit_pairs, inv_std, normed = by_groups(
        forward_rows, (pair_blk, bucket_blk), group_rows
    )
    bias_tile = lax.all_to_all(bias_vals, "heads", split_axis=1, concat_axis=0, tiled=True)
    scores = jnp.einsum(
        "hdi,hdj->ihj", q_heads, k_heads, preferred_element_type=jnp.float32
    ) * score_scale + bias_tile.astype(jnp.float32)
    attn_probs = jnp.where((key_mask == 1)[None, None, :], jnp.exp(scores - norm_cols), 0.0)
    probs_low = attn_probs.astype(jnp.bfloat16)
    dprobs = jnp.einsum("hdi,hdj->ihj", dout_heads, v_heads, preferred_element_type=jnp.float32)
    dscores = (attn_probs * (dprobs - delta_cols)).astype(jnp.bfloat16)
    dv_part = jnp.einsum("hdi,ihj->hdj", dout_heads, probs_low, preferred_element_type=jnp.float32)
    dk_part = jnp.einsum("hdi,ihj->hdj", q_heads, dscores, preferred_element_type=jnp.float32)
    dq_part = jnp.einsum("hdj,ihj->hdi", k_heads, dscores, preferred_element_type=jnp.float32)
    returned = lax.all_to_all(dscores, "heads", split_axis=0, concat_axis=1, tiled=True)
    grad_blk = by_groups(backward_rows, (unit_pairs, inv_std, normed, returned), group_rows)
    results = [(grad_blk, dk_part, dv_part, dq_part)]
    grad_pairs = jnp.concatenate([outcome[0] for outcome in results], axis=2)
    dk_cat = jnp.concatenate([outcome[1] for outcome in results], axis=2)
    dv_cat = jnp.concatenate([outcome[2] for outcome in results], axis=2)
    dq_total = results[0][3]
    dk_sum, dv_sum = lax.psum((dk_cat, dv_cat), "query")
    dq_sum = lax.psum(dq_total, "key")
    grad_q = (dq_sum * score_scale).astype(jnp.bfloat16)
    grad_k = (dk_sum * score_scale).astype(jnp.bfloat16)
    grad_v = dv_sum.astype(jnp.bfloat16)
    return (grad_pairs, grad_q, grad_k, grad_v)


def solution(mesh):
    return jax.shard_map(
        per_device,
        mesh=mesh,
        in_specs=(
            P(("query", "heads"), None, "key"),
            P(("query", "heads"), "key"),
            P(),
            P(),
            P(),
            P(),
            P(),
            P("key"),
            P("heads", None, "query"),
            P("heads", None, "key"),
            P("heads", None, "key"),
            P("heads", None, "query"),
            P("heads", None, "query"),
            P("heads", "query"),
        ),
        out_specs=(
            P(("query", "heads"), None, "key"),
            P("heads", None, "query"),
            P("heads", None, "key"),
            P("heads", None, "key"),
        ),
        check_vma=False,
    )
```

profile of v0, /device:TPU:1, one launch (start us, length us, event | category | flops | bytes accessed | tf_op | source)
XLA Modules:
  0.0 328.6 jit_solution(2500783627409047054)
XLA Ops:
  9.1 1.6 broadcast.105.clone
  10.7 22.6 %while.26 = (s32[]{:T(128)}, bf16[4,4,32,1024]{3,2,1,0:T(8,128)(2,1)}, f32[4,4,64,1024]{3,2,1,0:T(8,128)}, f32[4,4,1,1024]{3,1,2,0:T(4,128)S(1)}, bf16[4,4,64,10...) while((s32[]{:T(128)}, ...), condition=%wide.region_3.4_spmd, body=%wide.region_0.3_spmd.sunk | while | flops 221392896 | bytes 5854109 | solution.py:31
  11.3 2.9 fusion.120
  16.9 2.9 fusion.120
  22.6 2.9 fusion.120
  28.2 2.9 fusion.120
  33.3 2.8 copy.39
  36.1 17.0 %all-to-all-start = ((bf16[16,32,1024]{2,0,1:T(8,128)(2,1)}), bf16[16,32,1024]{2,0,1:T(8,128)(2,1)S(1)}, u32[]{:S(2)}, u32[]{:S(2)}) async-start(bf16[16,32,1024]{2,0,1:T(8,128)(2,1)} %copy.39), calls=%async_computation | async-start | bytes 2097152 | tf_op jit(solution)/shard_map/all_to_all | solution.py:96
  53.2 53.1 %all-to-all-done = bf16[16,32,1024]{2,0,1:T(8,128)(2,1)S(1)} async-done(((bf16[16,32,1024]{2,0,1:T(8,128)(2,1)}), bf16[16,32,1024]{2,0,1:T(8,128)(2,1)S(1)}, u32[]{:S(2)}, u32[]{:S(2)}) %all-to-all-start) | async-done | bytes 1048608 | tf_op jit(solution)/shard_map/all_to_all | solution.py:96
  106.6 1.9 copy.34
  108.4 2.3 fusion.80
  111.7 2.1 reduce.2
  113.8 2.3 copy.42
  116.1 2.6 reshape.144
  118.7 5.6 %all-to-all-start.1 = ((bf16[32,2,8192]{2,1,0:T(2,128)(2,1)}), bf16[32,2,8192]{2,1,0:T(2,128)(2,1)}, u32[]{:S(2)}, u32[]{:S(2)}) async-start(bf16[32,2,8192]{2,1,0:T(2,128)(2,1)} %reshape.144), calls=%async_computation.1 | async-start | bytes 2097152 | tf_op jit(solution)/shard_map/all_to_all | solution.py:107
  126.9 5.4 %all-reduce.7 = bf16[1,32,1024]{2,1,0:T(8,128)(2,1)} all-reduce(f32[1,32,1024]{2,1,0:T(8,128)S(1)} %convolution_bitcast_fusion), channel_id=1, replica_groups=mesh['query'=2,'key'=8,'heads'=32] {'query'}, use_global_device_ids=true, to_apply=%region_11.12 | all-reduce | flops 32768 | bytes 196608 | tf_op jit(solution)/shard_map/psum | solution.py:114
  132.3 90.8 %all-reduce.4.cloned.1.call-done = f32[1,32,512]{2,1,0:T(8,128)} async-done(((f32[1,32,512]{2,1,0:T(8,128)}), f32[1,32,512]{2,1,0:T(8,128)}) %all-reduce.4.cloned.1.call-update) | async-done | bytes 65552 | tf_op jit(solution)/shard_map/psum | solution.py:115
  224.5 45.3 %all-reduce.6.cloned.1.call-done = f32[1,32,1024]{2,1,0:T(8,128)} async-done(((f32[1,32,1024]{2,1,0:T(8,128)}), f32[1,32,1024]{2,1,0:T(8,128)}) %all-reduce.6.cloned.1.call-update) | async-done | bytes 131088 | tf_op jit(solution)/shard_map/psum | solution.py:114
  269.8 1.5 multiply_convert_fusion
  271.3 4.3 %reshape.145 = bf16[512,1,1024]{2,1,0:T(2,128)(2,1)S(1)} reshape(bf16[32,2,8192]{2,1,0:T(2,128)(2,1)} %all-to-all-done.1) | data formatting | bytes 2097152
  276.0 1.6 copy.40
  277.9 42.5 %while.27 = (s32[]{:T(128)}, bf16[4,4,64,1024]{3,2,1,0:T(8,128)(2,1)S(1)}, f32[4,4,1,1024]{3,1,2,0:T(4,128)S(1)}, bf16[4,4,32,1024]{3,2,1,0:T(8,128)(2,1)}, bf16...) while((s32[]{:T(128)}, ...), condition=%wide.region_8.9_spmd, body=%wide.region_5.8_spmd.sunk | while | flops 349437952 | bytes 14158209 | solution.py:31
  278.0 3.8 %fusion.127 = f32[4,1024,256]{2,1,0:T(8,128)} fusion(bf16[4,4,64,1024]{3,2,1,0:T(8,128)(2,1)} %get-tuple-element.441, s32[]{:T(128)S(6)} %copy.65, bf16[64,256]{1,0:T(8,128)(2,1)S(1)} %get-tuple-element.442), kind=kOutput, calls=%fused_computation.65.clone.1 | convolution fusion | flops 134217728 | bytes 4751364 | tf_op jit(solution)/shard_map/while/body/eval_jaxpr/rck,cf->rfk/dot_general | solution.py:77
  281.7 5.3 %fusion.128 = (f32[4,1024]{1,0:T(4,128)S(1)}, f32[4,1024]{1,0:T(4,128)S(1)}, f32[4,64,1024]{2,1,0:T(8,128)S(1)}) fusion(f32[4,4,64,1024]{3,2,1,0:T(8,128)} %get-tuple-element.445, s32[]{:T(128)S(6)} %copy.65, f32[64]{0:T(128)S(1)} %get-tuple-element.444, bf16[64,256]{1,0:T(8,128)(2,1)S(1)} %get-tuple-element.442, f32[4,1024,256]{2,1,0:T(8,128)} %fusion.127, ...), kind=kOutput, calls=%fused_computation.109.clone.1 | convolution fusion | flops 213901312 | bytes 6637824 | tf_op jit(solution)/shard_map/while/body/eval_jaxpr/rfk,cf->rck/dot_general | solution.py:84
  287.1 1.5 fusion.129
  288.6 3.8 %fusion.127 = f32[4,1024,256]{2,1,0:T(8,128)} fusion(bf16[4,4,64,1024]{3,2,1,0:T(8,128)(2,1)} %get-tuple-element.441, s32[]{:T(128)S(6)} %copy.65, bf16[64,256]{1,0:T(8,128)(2,1)S(1)} %get-tuple-element.442), kind=kOutput, calls=%fused_computation.65.clone.1 | convolution fusion | flops 134217728 | bytes 4751364 | tf_op jit(solution)/shard_map/while/body/eval_jaxpr/rck,cf->rfk/dot_general | solution.py:77
  292.3 5.3 %fusion.128 = (f32[4,1024]{1,0:T(4,128)S(1)}, f32[4,1024]{1,0:T(4,128)S(1)}, f32[4,64,1024]{2,1,0:T(8,128)S(1)}) fusion(f32[4,4,64,1024]{3,2,1,0:T(8,128)} %get-tuple-element.445, s32[]{:T(128)S(6)} %copy.65, f32[64]{0:T(128)S(1)} %get-tuple-element.444, bf16[64,256]{1,0:T(8,128)(2,1)S(1)} %get-tuple-element.442, f32[4,1024,256]{2,1,0:T(8,128)} %fusion.127, ...), kind=kOutput, calls=%fused_computation.109.clone.1 | convolution fusion | flops 213901312 | bytes 6637824 | tf_op jit(solution)/shard_map/while/body/eval_jaxpr/rfk,cf->rck/dot_general | solution.py:84
  297.7 1.5 fusion.129
  299.2 3.8 %fusion.127 = f32[4,1024,256]{2,1,0:T(8,128)} fusion(bf16[4,4,64,1024]{3,2,1,0:T(8,128)(2,1)} %get-tuple-element.441, s32[]{:T(128)S(6)} %copy.65, bf16[64,256]{1,0:T(8,128)(2,1)S(1)} %get-tuple-element.442), kind=kOutput, calls=%fused_computation.65.clone.1 | convolution fusion | flops 134217728 | bytes 4751364 | tf_op jit(solution)/shard_map/while/body/eval_jaxpr/rck,cf->rfk/dot_general | solution.py:77
  303.0 5.3 %fusion.128 = (f32[4,1024]{1,0:T(4,128)S(1)}, f32[4,1024]{1,0:T(4,128)S(1)}, f32[4,64,1024]{2,1,0:T(8,128)S(1)}) fusion(f32[4,4,64,1024]{3,2,1,0:T(8,128)} %get-tuple-element.445, s32[]{:T(128)S(6)} %copy.65, f32[64]{0:T(128)S(1)} %get-tuple-element.444, bf16[64,256]{1,0:T(8,128)(2,1)S(1)} %get-tuple-element.442, f32[4,1024,256]{2,1,0:T(8,128)} %fusion.127, ...), kind=kOutput, calls=%fused_computation.109.clone.1 | convolution fusion | flops 213901312 | bytes 6637824 | tf_op jit(solution)/shard_map/while/body/eval_jaxpr/rfk,cf->rck/dot_general | solution.py:84
  309.8 3.8 %fusion.127 = f32[4,1024,256]{2,1,0:T(8,128)} fusion(bf16[4,4,64,1024]{3,2,1,0:T(8,128)(2,1)} %get-tuple-element.441, s32[]{:T(128)S(6)} %copy.65, bf16[64,256]{1,0:T(8,128)(2,1)S(1)} %get-tuple-element.442), kind=kOutput, calls=%fused_computation.65.clone.1 | convolution fusion | flops 134217728 | bytes 4751364 | tf_op jit(solution)/shard_map/while/body/eval_jaxpr/rck,cf->rfk/dot_general | solution.py:77
  313.6 5.3 %fusion.128 = (f32[4,1024]{1,0:T(4,128)S(1)}, f32[4,1024]{1,0:T(4,128)S(1)}, f32[4,64,1024]{2,1,0:T(8,128)S(1)}) fusion(f32[4,4,64,1024]{3,2,1,0:T(8,128)} %get-tuple-element.445, s32[]{:T(128)S(6)} %copy.65, f32[64]{0:T(128)S(1)} %get-tuple-element.444, bf16[64,256]{1,0:T(8,128)(2,1)S(1)} %get-tuple-element.442, f32[4,1024,256]{2,1,0:T(8,128)} %fusion.127, ...), kind=kOutput, calls=%fused_computation.109.clone.1 | convolution fusion | flops 213901312 | bytes 6637824 | tf_op jit(solution)/shard_map/while/body/eval_jaxpr/rfk,cf->rck/dot_general | solution.py:84
  (93 shorter events, 22.8 us)
Async XLA Ops:
  7.2 101.3 %copy-start = (bf16[1,32,1024]{2,1,0:T(8,128)(2,1)S(1)}, bf16[1,32,1024]{2,1,0:T(8,128)(2,1)}, u32[]{:S(2)}) copy-start(bf16[1,32,1024]{2,1,0:T(8,128)(2,1)} %param.27) | copy-start | bytes 196612
  7.2 3.5 %copy-start.11 = (bf16[256,32]{0,1:T(8,128)(2,1)S(1)}, bf16[256,32]{0,1:T(8,128)(2,1)}, u32[]{:S(2)}) copy-start(bf16[256,32]{0,1:T(8,128)(2,1)} %param.23) | copy-start | bytes 49156
  7.2 3.5 %copy-start.12 = (f32[256]{0:T(256)S(1)}, f32[256]{0:T(256)}, u32[]{:S(2)}) copy-start(f32[256]{0:T(256)} %param.22) | copy-start | bytes 3076
  7.2 3.4 %copy-start.3 = (bf16[64,256]{1,0:T(8,128)(2,1)S(1)}, bf16[64,256]{1,0:T(8,128)(2,1)}, u32[]{:S(2)}) copy-start(bf16[64,256]{1,0:T(8,128)(2,1)} %param.21) | copy-start | bytes 98308
  7.2 3.4 %copy-start.8 = (f32[64]{0:T(128)S(1)}, f32[64]{0:T(128)}, u32[]{:S(2)}) copy-start(f32[64]{0:T(128)} %param.20) | copy-start | bytes 772
  7.2 3.4 %copy-start.1 = (bf16[16,64,1024]{2,1,0:T(8,128)(2,1)S(1)}, bf16[16,64,1024]{2,1,0:T(8,128)(2,1)}, u32[]{:S(2)}) copy-start(bf16[16,64,1024]{2,1,0:T(8,128)(2,1)} %param.18) | copy-start | bytes 6291460
  33.3 19.9 %copy-start.4 = (bf16[1,32,512]{2,1,0:T(8,128)(2,1)S(1)}, bf16[1,32,512]{2,1,0:T(8,128)(2,1)}, u32[]{:S(2)}) copy-start(bf16[1,32,512]{2,1,0:T(8,128)(2,1)} %param.30) | copy-start | bytes 98308
  33.3 19.9 %copy-start.7 = (bf16[1,32,512]{2,1,0:T(8,128)(2,1)S(1)}, bf16[1,32,512]{2,1,0:T(8,128)(2,1)}, u32[]{:S(2)}) copy-start(bf16[1,32,512]{2,1,0:T(8,128)(2,1)} %param.29) | copy-start | bytes 98308
  33.3 19.9 %copy-start.9 = (s32[1024]{0:T(1024)S(1)}, s32[1024]{0:T(1024)}, u32[]{:S(2)}) copy-start(s32[1024]{0:T(1024)} %param.25) | copy-start | bytes 12292
  36.1 70.2 %all-to-all-start = ((bf16[16,32,1024]{2,0,1:T(8,128)(2,1)}), bf16[16,32,1024]{2,0,1:T(8,128)(2,1)S(1)}, u32[]{:S(2)}, u32[]{:S(2)}) async-start(bf16[16,32,1024]{2,0,1:T(8,128)(2,1)} %copy.39), calls=%async_computation | async-start | bytes 2097152 | tf_op jit(solution)/shard_map/all_to_all | solution.py:96
  106.5 1.9 copy-start.5
  106.5 1.9 copy-start.10
  108.4 2.3 copy-start.6
  118.7 152.6 %all-to-all-start.1 = ((bf16[32,2,8192]{2,1,0:T(2,128)(2,1)}), bf16[32,2,8192]{2,1,0:T(2,128)(2,1)}, u32[]{:S(2)}, u32[]{:S(2)}) async-start(bf16[32,2,8192]{2,1,0:T(2,128)(2,1)} %reshape.144), calls=%async_computation.1 | async-start | bytes 2097152 | tf_op jit(solution)/shard_map/all_to_all | solution.py:107
  124.4 98.7 %all-reduce.4.cloned.1.call-start = ((), (), s32[]{:S(2)}) async-start(), calls=%async_computation.2 | async-start | bytes 131072 | tf_op jit(solution)/shard_map/psum | solution.py:115
  125.3 144.4 %all-reduce.6.cloned.1.call-start = ((), (), s32[]{:S(2)}) async-start(), calls=%async_computation.3 | async-start | bytes 262144 | tf_op jit(solution)/shard_map/psum | solution.py:114
  320.4 1.3 copy-start.2
Sparse Core Ops, SparseCore 0:
  128.7 94.3 all-reduce.3
  226.2 43.5 all-reduce.5
where the time goes:
time: 330 us; the launch traced here: 329 us
  waiting for transfers between devices  189 us (57%)
  matrix products  54.1 us (16%)
  starting transfers between devices  22.8 us (7%)
  local copies, waits for them, and re-layouts  21.5 us (7%)
  other arithmetic  21.1 us (6%)
  between operations  14.3 us (4%)
  blocking collectives  5.39 us (2%)
    psum x1, waiting for transfers between devices, per_device(): dq_sum = lax.psum(dq_total, 'key')  90.8 us
    all_to_all x1, waiting for transfers between devices, per_device(): lax.all_to_all(bias_vals, 'heads', split_axis=1, concat_axis=0, tiled=True)  53.1 us
    psum x1, waiting for transfers between devices, per_device(): dk_sum, dv_sum = lax.psum((dk_cat, dv_cat), 'query')  45.3 us
    dot_general x4, matrix products, backward_rows(): jnp.einsum('rfk,cf->rck', dpre, w_in, preferred_element_type=jnp.float32)  21.4 us
    all_to_all x1, starting transfers between devices, per_device(): lax.all_to_all(bias_vals, 'heads', split_axis=1, concat_axis=0, tiled=True)  17 us
    dot_general x4, matrix products, backward_rows(): jnp.einsum('rck,cf->rfk', normed, w_in, preferred_element_type=jnp.float32)  15 us
    dynamic_update_slice x16, other arithmetic, by_groups(): result = lax.map(lambda blocks: kernel_fn(*blocks), stacked)  14.5 us
    dot_general x4, matrix products, forward_rows(): jnp.einsum('rfk,fh->rhk', hidden, w_out, preferred_element_type=jnp.float32)  11.7 us
  transfers between devices with their start and end apart: 4, of which 3 were waited for; matrix products, arithmetic and copies ran while one was open for 2% of the time, Pallas kernels for 0%

commit v1 on v0

v1 whole, which is shorter than its diff:
```python
import functools
import math

import jax
import jax.numpy as jnp
from jax import lax
from jax.experimental import pallas as pl
from jax.experimental.pallas import tpu as pltpu
from jax.sharding import PartitionSpec as P

F32 = jnp.float32
BF16 = jnp.bfloat16
MESH = pl.DeviceIdType.MESH


def dot(lhs, rhs):
    return jnp.dot(lhs, rhs, preferred_element_type=F32)


def iota(shape, axis):
    return lax.broadcasted_iota(jnp.int32, shape, axis)


def ones_where(cond):
    return jnp.where(cond, 1.0, 0.0).astype(BF16)


def column(row):
    size = row.shape[1]
    diag = iota((size, size), 0) == iota((size, size), 1)
    return jnp.sum(jnp.where(diag, jnp.broadcast_to(row, (size, size)), 0.0), axis=1, keepdims=True)


def pieces(value):
    first = value.astype(BF16).astype(F32)
    second = (value - first).astype(BF16).astype(F32)
    third = (value - first - second).astype(BF16).astype(F32)
    return first, second, third


def gelu_parts(pre_act):
    cdf_val = 0.5 * (1.0 + lax.erf(pre_act * (1.0 / math.sqrt(2.0))))
    density = jnp.exp(-0.5 * pre_act * pre_act) * (1.0 / math.sqrt(2.0 * math.pi))
    return pre_act * cdf_val, cdf_val + pre_act * density


def kernel(
    x_hbm, bucket_hbm, gain_hbm, win_hbm, bin_hbm, woutt_hbm, table_hbm, mask_hbm,
    q_hbm, k_hbm, v_hbm, out_hbm, dout_hbm, norm_hbm,
    gp_hbm, gq_hbm, gk_hbm, gv_hbm,
    x_v, bucket_v, gain_v, win_v, bin_v, woutt_v, table_v, mask_v,
    q_v, out_v, dout_v, norm_v,
    gp_v, gq_v, gkv_v,
    slope_v, stat_v, kv_v, bias_out, bias_in, ds_all, ds_in, probs_v,
    qstage, qrecv, qblk_v, doblk_v, norm_b, delta_b, dkv_v,
    rsp_send, rsp_recv, rsm_send, rsm_recv,
    dq_send, dq_recv, dq_peers, w1_v, w2_v, wmix_v, tab_v,
    in_sem, x_sem, kv_sem, gp_sem, o_sem,
    ag_send, ag_recv, q_send, q_recv, b_send, b_recv, d_send, d_recv,
    rp_send, rp_recv, rm_send, rm_recv, f_send, f_recv,
    p1_send, p1_recv, p2_send, p2_recv,
):
    core = lax.axis_index("query")
    key = lax.axis_index("key")
    col = lax.axis_index("heads")
    zpos = col // 2
    ypos = col % 2
    home = zpos // 8
    slot = zpos % 8
    mine = core * 2 + ypos
    is_home = home == core
    score_scale = 1.0 / math.sqrt(32.0)

    def device(core_at, z_at, y_at):
        return (core_at, key, z_at * 2 + y_at)

    right = device(core, (zpos + 1) % 16, ypos)
    left = device(core, (zpos + 15) % 16, ypos)

    def quad(step):
        core_at = (core + step // 2) % 2
        y_at = (ypos + step % 2) % 2
        return device(core_at, zpos, y_at), core_at * 2 + y_at

    barrier = pltpu.get_barrier_semaphore()

    def greet(where):
        pl.semaphore_signal(barrier, inc=1, device_id=where, device_id_type=MESH)

    greet(right)
    greet(left)
    for step in (1, 2, 3):
        greet(quad(step)[0])

    def greet_z(at, carry):
        @pl.when(jnp.logical_not(jnp.logical_and(is_home, at == zpos)))
        def _():
            greet(device(home, at, ypos))

        @pl.when(jnp.logical_not(jnp.logical_and(core == at // 8, core * 8 + at % 8 == zpos)))
        def _():
            greet(device(at // 8, core * 8 + at % 8, ypos))

        return carry

    lax.fori_loop(0, 16, greet_z, 0)

    def greet_key(step, carry):
        greet((core, (key + step) % 8, col))
        return carry

    lax.fori_loop(1, 8, greet_key, 0)

    loads = [
        pltpu.make_async_copy(src, dst, in_sem.at[at])
        for at, (src, dst) in enumerate(
            (
                (gain_hbm, gain_v), (win_hbm, win_v), (bin_hbm, bin_v), (woutt_hbm, woutt_v),
                (table_hbm, table_v), (bucket_hbm, bucket_v), (mask_hbm, mask_v), (q_hbm, q_v),
                (out_hbm, out_v), (dout_hbm, dout_v), (norm_hbm, norm_v),
            )
        )
    ]
    for load in loads:
        load.start()

    def x_load(pair):
        return pltpu.make_async_copy(x_hbm.at[pl.ds(pair * 2, 2)], x_v.at[pl.ds(pair * 2, 2)], x_sem.at[pair])

    for pair in range(8):
        x_load(pair).start()

    k_load = pltpu.make_async_copy(k_hbm.at[0], kv_v.at[slot, pl.ds(0, 32)], kv_sem.at[0])
    v_load = pltpu.make_async_copy(v_hbm.at[0], kv_v.at[slot, pl.ds(32, 32)], kv_sem.at[1])

    @pl.when(is_home)
    def _():
        k_load.start()
        v_load.start()

    for load in loads:
        load.wait()

    sel_row = iota((32, 32), 0)
    part_at, head_at = sel_row // 8, sel_row % 8
    head_of = 2 * (8 * (part_at // 2) + head_at) + part_at % 2
    select = ones_where(iota((32, 32), 1) == head_of)
    woutt = woutt_v[...]
    wmix_v[...] = dot(select, woutt).astype(BF16)
    tab_v[...] = dot(select, table_v[...].T).astype(BF16)
    row64 = iota((64, 32), 0)
    part64, head64 = row64 // 16, row64 % 8
    head_of64 = 2 * (8 * (part64 // 2) + head64) + part64 % 2
    spread = dot(ones_where(iota((64, 32), 1) == head_of64), woutt).T
    parity = (iota((256, 64), 1) // 8) % 2
    w2_v[0:256, :] = jnp.where(parity == 0, spread, 0.0).astype(BF16)
    w2_v[256:512, :] = jnp.where(parity == 1, spread, 0.0).astype(BF16)
    win_t = win_v[...].astype(F32).T
    zero = jnp.zeros((256, 64), F32)
    w1_v[0:256, :] = jnp.concatenate([win_t, zero], axis=1).astype(BF16)
    w1_v[256:512, :] = jnp.concatenate([zero, win_t], axis=1).astype(BF16)
    gain_col = column(gain_v[...])
    bin_col = column(bin_v[...])

    dout_f = dout_v[0].astype(F32)
    delta = jnp.sum(dout_f * out_v[0].astype(F32), axis=0, keepdims=True)
    n0, n1, n2 = pieces(norm_v[...])
    d0, d1, d2 = pieces(delta)
    sub = iota((64, 512), 0)
    extra = jnp.zeros((64, 512), F32)
    for at, piece in enumerate((n0, n1, n2, d0, d1, d2)):
        extra = jnp.where(sub == at, jnp.broadcast_to(piece, (64, 512)), extra)
    packed = jnp.concatenate([q_v[0].astype(F32), dout_f, extra], axis=0)
    qstage[...] = packed.T.astype(BF16).reshape(16, 32, 128)

    def q_copy(at):
        return pltpu.make_async_remote_copy(
            src_ref=qstage.at[at], dst_ref=qrecv.at[slot * 2 + core], send_sem=q_send.at[at],
            recv_sem=q_recv.at[slot * 2 + core], device_id=device(home, at, ypos), device_id_type=MESH,
        )

    def q_arrival(at):
        return pltpu.make_async_remote_copy(
            src_ref=qstage.at[0], dst_ref=qrecv.at[at], send_sem=q_send.at[0],
            recv_sem=q_recv.at[at], device_id=device(at % 2, core * 8 + at // 2, ypos), device_id_type=MESH,
        )

    def ag_copy(at, way, where):
        return pltpu.make_async_remote_copy(
            src_ref=kv_v.at[at], dst_ref=kv_v.at[at], send_sem=ag_send.at[way, at],
            recv_sem=ag_recv.at[at], device_id=where, device_id_type=MESH,
        )

    def ag_step(step):
        from_left = (zpos + 16 - step) % 16
        from_right = (zpos + step) % 16

        @pl.when(jnp.logical_and(step <= 8, from_left // 8 == core))
        def _():
            ag_copy(from_left % 8, 0, right).wait_recv()

            @pl.when(step < 8)
            def _():
                ag_copy(from_left % 8, 0, right).start()

        @pl.when(jnp.logical_and(step <= 7, from_right // 8 == core))
        def _():
            ag_copy(from_right % 8, 1, left).wait_recv()

            @pl.when(step < 7)
            def _():
                ag_copy(from_right % 8, 1, left).start()

    def ag_drain(step, carry):
        from_left = (zpos + 16 - step) % 16
        from_right = (zpos + step) % 16

        @pl.when(jnp.logical_and(step < 8, from_left // 8 == core))
        def _():
            ag_copy(from_left % 8, 0, right).wait_send()

        @pl.when(jnp.logical_and(step < 7, from_right // 8 == core))
        def _():
            ag_copy(from_right % 8, 1, left).wait_send()

        return carry

    def bias_copy(step, pair):
        where, part = quad(step)
        return pltpu.make_async_remote_copy(
            src_ref=bias_out.at[part, pair], dst_ref=bias_in.at[mine, pair], send_sem=b_send.at[step],
            recv_sem=b_recv.at[mine], device_id=where, device_id_type=MESH,
        )

    def bias_all(step):
        where, part = quad(step)
        return pltpu.make_async_remote_copy(
            src_ref=bias_out.at[part], dst_ref=bias_in.at[part], send_sem=b_send.at[step],
            recv_sem=b_recv.at[part], device_id=where, device_id_type=MESH,
        )

    def forward_pair(pair):
        x_load(pair).wait()
        mats = []
        for r in range(2):
            values = x_v[pair * 2 + r].astype(F32)
            mean = jnp.sum(values, axis=0, keepdims=True) * (1.0 / 64.0)
            centre = values - mean
            inv_std = lax.rsqrt(jnp.sum(centre * centre, axis=0, keepdims=True) * (1.0 / 64.0) + 1e-05)
            stat_v[pair * 2 + r, 0:1, :] = mean
            stat_v[pair * 2 + r, 1:2, :] = inv_std
            mats.append((centre * inv_std * gain_col).astype(BF16))
        pre = dot(w1_v[...], jnp.concatenate(mats, axis=0))
        mixes = []
        for r in range(2):
            gelu_val, gelu_slope = gelu_parts(pre[r * 256:(r + 1) * 256] + bin_col)
            slope_v[pair * 2 + r] = gelu_slope.astype(BF16)
            hidden = gelu_val.astype(BF16)
            onehot = ones_where(bucket_v[pl.ds(pair * 2 + r, 1), :] == iota((32, 1024), 0))
            mixes.append(dot(wmix_v[...], hidden) + dot(tab_v[...], onehot))
        for part in range(4):
            rows = [mix[part * 8:(part + 1) * 8] for mix in mixes]
            bias_out[part, pair] = jnp.concatenate(rows, axis=0).astype(BF16)

    forward_pair(0)

    @pl.when(is_home)
    def _():
        pl.semaphore_wait(barrier, 42)

    @pl.when(jnp.logical_not(is_home))
    def _():
        pl.semaphore_wait(barrier, 44)

    @pl.when(is_home)
    def _():
        k_load.wait()
        v_load.wait()
        ag_copy(slot, 0, right).start()
        ag_copy(slot, 1, left).start()
        qrecv[slot * 2 + core] = qstage[zpos]

    def q_start(at, carry):
        @pl.when(jnp.logical_not(jnp.logical_and(is_home, at == zpos)))
        def _():
            q_copy(at).start()

        return carry

    lax.fori_loop(0, 16, q_start, 0)
    for step in (1, 2, 3):
        bias_copy(step, 0).start()

    def forward_body(pair, carry):
        forward_pair(pair)
        for step in (1, 2, 3):
            bias_copy(step, pair).start()
        ag_step(pair)
        return carry

    lax.fori_loop(1, 8, forward_body, 0)

    def q_wait(at, carry):
        @pl.when(jnp.logical_not(jnp.logical_and(at % 2 == core, core * 8 + at // 2 == zpos)))
        def _():
            q_arrival(at).wait_recv()

        return carry

    lax.fori_loop(0, 16, q_wait, 0)
    arrived = qrecv[...].reshape(512, 128)
    row_a, row_b = iota((512, 512), 0), iota((512, 512), 1)
    order = ones_where(jnp.logical_and(row_a // 8 == row_b % 64, row_a % 8 == row_b // 64))
    by_row = dot(order, arrived).astype(BF16)
    lane, spot = iota((128, 256), 0), iota((128, 256), 1)
    own_head = iota((512, 256), 0) % 8 == iota((512, 256), 1) // 32
    qblk_v[...] = jnp.where(own_head, dot(by_row, ones_where(lane == spot % 32)), 0.0).astype(BF16)
    doblk_v[...] = jnp.where(own_head, dot(by_row, ones_where(lane == 32 + spot % 32)), 0.0).astype(BF16)
    wide = iota((128, 128), 0)
    norm_b[...] = dot(by_row, ones_where(jnp.logical_and(wide >= 64, wide < 67)))
    delta_b[...] = dot(by_row, ones_where(jnp.logical_and(wide >= 67, wide < 70)))

    ag_step(8)
    live = mask_v[...] == 1
    keys = kv_v[:, 0:32, :].reshape(256, 1024)
    values = kv_v[:, 32:64, :].reshape(256, 1024)

    def ds_copy(step):
        where, part = quad(step)
        return pltpu.make_async_remote_copy(
            src_ref=ds_all.at[part], dst_ref=ds_in.at[mine], send_sem=d_send.at[step],
            recv_sem=d_recv.at[mine], device_id=where, device_id_type=MESH,
        )

    def ds_arrival(step):
        where, part = quad(step)
        return pltpu.make_async_remote_copy(
            src_ref=ds_all.at[part], dst_ref=ds_in.at[part], send_sem=d_send.at[step],
            recv_sem=d_recv.at[part], device_id=where, device_id_type=MESH,
        )

    for step in (1, 2, 3, 0):
        _, part = quad(step)
        if step:
            bias_all(step).wait_recv()
            bias = bias_in[part]
        else:
            bias = bias_out[part]
        rows = pl.ds(pl.multiple_of(part * 128, 128), 128)
        scores = dot(qblk_v[rows, :], keys) * score_scale + bias.reshape(128, 1024).astype(F32)
        shift = jnp.concatenate([norm_b[rows, :]] * 8, axis=1)
        probs = jnp.where(live, jnp.exp(scores - shift), 0.0)
        probs_v[rows, :] = probs.astype(BF16)
        less = jnp.concatenate([delta_b[rows, :]] * 8, axis=1)
        dscores = (probs * (dot(doblk_v[rows, :], values) - less)).astype(BF16)
        ds_all[part] = dscores
        if step:
            ds_copy(step).start()
        else:
            ds_in[part] = dscores

    ds_flat = ds_all[...].reshape(512, 1024)
    dkv_v[:, 0:32, :] = dot(qblk_v[...].T, ds_flat).reshape(8, 32, 1024)
    dkv_v[:, 32:64, :] = dot(doblk_v[...].T, probs_v[...]).reshape(8, 32, 1024)

    def rs_plus(step):
        return pltpu.make_async_remote_copy(
            src_ref=rsp_send.at[step], dst_ref=rsp_recv.at[step], send_sem=rp_send.at[step],
            recv_sem=rp_recv.at[step], device_id=right, device_id_type=MESH,
        )

    def rs_minus(step):
        return pltpu.make_async_remote_copy(
            src_ref=rsm_send.at[step], dst_ref=rsm_recv.at[step], send_sem=rm_send.at[step],
            recv_sem=rm_recv.at[step], device_id=left, device_id_type=MESH,
        )

    def to_right(step):
        return (zpos + 8 - step) % 16

    def to_left(step):
        return (zpos + 9 + step) % 16

    @pl.when(to_right(0) // 8 == core)
    def _():
        rsp_send[0] = dkv_v[to_right(0) % 8].astype(BF16)
        rs_plus(0).start()

    @pl.when(to_left(0) // 8 == core)
    def _():
        rsm_send[0] = dkv_v[to_left(0) % 8].astype(BF16)
        rs_minus(0).start()

    def rs_step(step):
        @pl.when(jnp.logical_and(step < 8, to_right(step) // 8 == core))
        def _():
            rs_plus(step - 1).wait_recv()
            rsp_send[step] = (rsp_recv[step - 1].astype(F32) + dkv_v[to_right(step) % 8]).astype(BF16)
            rs_plus(step).start()

        @pl.when(jnp.logical_and(step < 7, to_left(step) // 8 == core))
        def _():
            rs_minus(step - 1).wait_recv()
            rsm_send[step] = (rsm_recv[step - 1].astype(F32) + dkv_v[to_left(step) % 8]).astype(BF16)
            rs_minus(step).start()

    dq_full = lax.dot_general(ds_flat, keys, (((1,), (1,)), ((), ())), preferred_element_type=F32)
    dq_full = jnp.where(own_head, dq_full, 0.0)
    dq_fold = dq_full[:, 0:128] + dq_full[:, 128:256]
    dq_fold = dq_fold + pltpu.roll(dq_fold, 64, 1)
    dq_fold = dq_fold + pltpu.roll(dq_fold, 32, 1)
    group = iota((512, 128), 1) // 32
    h0, h1, h2 = pieces(dq_fold)
    dq_split = jnp.where(group == 0, h0, jnp.where(group == 1, h1, jnp.where(group == 2, h2, 0.0))).astype(BF16)
    back = ones_where(jnp.logical_and(row_b // 8 == row_a % 64, row_b % 8 == row_a // 64))
    dq_head = dot(back, dq_split)
    dq_head = dq_head + pltpu.roll(dq_head, 64, 1)
    dq_head = dq_head + pltpu.roll(dq_head, 32, 1)
    dq_head = dq_head.reshape(16, 32, 128)
    group8 = iota((16, 8, 128), 2) // 32
    dense = dq_head[:, 0:8, :]
    for at in range(1, 4):
        dense = jnp.where(group8 == at, dq_head[:, at * 8:(at + 1) * 8, :], dense)
    dq_send[...] = dense

    def p1_copy(at):
        return pltpu.make_async_remote_copy(
            src_ref=dq_send.at[at], dst_ref=dq_recv.at[zpos], send_sem=p1_send.at[at],
            recv_sem=p1_recv.at[zpos], device_id=device(at % 2, core * 8 + at // 2, ypos), device_id_type=MESH,
        )

    def p1_arrival(at):
        return pltpu.make_async_remote_copy(
            src_ref=dq_send.at[0], dst_ref=dq_recv.at[at], send_sem=p1_send.at[0],
            recv_sem=p1_recv.at[at], device_id=device(home, at, ypos), device_id_type=MESH,
        )

    def p1_start(at, carry):
        @pl.when(jnp.logical_not(jnp.logical_and(at % 2 == core, core * 8 + at // 2 == zpos)))
        def _():
            p1_copy(at).start()

        return carry

    lax.fori_loop(0, 16, p1_start, 0)

    @pl.when(is_home)
    def _():
        dq_recv[zpos] = dq_send[slot * 2 + core]

    def p2_copy(step):
        return pltpu.make_async_remote_copy(
            src_ref=dq_recv, dst_ref=dq_peers.at[key], send_sem=p2_send.at[step],
            recv_sem=p2_recv.at[key], device_id=(core, (key + step) % 8, col), device_id_type=MESH,
        )

    def p2_arrival(step):
        peer = (key + step) % 8
        return pltpu.make_async_remote_copy(
            src_ref=dq_recv, dst_ref=dq_peers.at[peer], send_sem=p2_send.at[step],
            recv_sem=p2_recv.at[peer], device_id=(core, peer, col), device_id_type=MESH,
        )

    def phase_two():
        def p1_wait(at, carry):
            @pl.when(jnp.logical_not(jnp.logical_and(is_home, at == zpos)))
            def _():
                p1_arrival(at).wait_recv()

            return carry

        lax.fori_loop(0, 16, p1_wait, 0)
        dq_peers[key] = dq_recv[...]

        def p2_start(step, carry):
            p2_copy(step).start()
            return carry

        lax.fori_loop(1, 8, p2_start, 0)

    for step in (1, 2, 3):
        ds_arrival(step).wait_recv()

    win = win_v[...]

    def gp_copy(pair):
        return pltpu.make_async_copy(gp_v.at[pl.ds(pair * 2, 2)], gp_hbm.at[pl.ds(pair * 2, 2)], gp_sem.at[pair])

    def backward_pair(pair):
        at = pl.ds(pl.multiple_of(pair * 16, 16), 16)
        dhidden = dot(w2_v[...], ds_in[:, at, :].reshape(64, 1024))
        for r in range(2):
            row = pair * 2 + r
            dpre = (dhidden[r * 256:(r + 1) * 256] * slope_v[row].astype(F32)).astype(BF16)
            dunit = dot(win, dpre) * gain_col
            inv_std = stat_v[row, 1:2, :]
            unit = (x_v[row].astype(F32) - stat_v[row, 0:1, :]) * inv_std
            first = jnp.sum(dunit, axis=0, keepdims=True) * (1.0 / 64.0)
            second = jnp.sum(dunit * unit, axis=0, keepdims=True) * (1.0 / 64.0)
            gp_v[row] = (inv_std * (dunit - first - unit * second)).astype(BF16)
        gp_copy(pair).start()

    def backward_body(pair, carry):
        backward_pair(pair)
        rs_step(pair + 1)

        @pl.when(pair == 3)
        def _():
            phase_two()

        return carry

    lax.fori_loop(0, 7, backward_body, 0)
    backward_pair(7)

    sibling, _ = quad(2)

    def f_copy():
        return pltpu.make_async_remote_copy(
            src_ref=gkv_v, dst_ref=gkv_v, send_sem=f_send, recv_sem=f_recv,
            device_id=sibling, device_id_type=MESH,
        )

    @pl.when(is_home)
    def _():
        rs_plus(7).wait_recv()
        rs_minus(6).wait_recv()
        total = dkv_v[slot] + rsp_recv[7].astype(F32) + rsm_recv[6].astype(F32)
        gkv_v[0:32, :] = (total[0:32] * score_scale).astype(BF16)
        gkv_v[32:64, :] = total[32:64].astype(BF16)
        f_copy().start()

    def p2_wait(step, carry):
        p2_arrival(step).wait_recv()
        return carry

    lax.fori_loop(1, 8, p2_wait, 0)
    total_q = dq_peers[0]
    for at in range(1, 8):
        total_q = total_q + dq_peers[at]
    final_q = (total_q.reshape(128, 128) * score_scale).astype(BF16).astype(F32).T.astype(BF16)
    lane_a, lane_b = iota((128, 512), 0), iota((128, 512), 1)
    grad_q = jnp.zeros((32, 512), F32)
    for at in range(4):
        place = jnp.logical_and(
            lane_a // 8 == lane_b // 32,
            jnp.logical_and(lane_a % 8 == lane_b % 8, (lane_b // 8) % 4 == at),
        )
        grad_q = grad_q + dot(final_q[at * 32:(at + 1) * 32, :], ones_where(place))
    gq_v[...] = grad_q.astype(BF16)
    gq_copy = pltpu.make_async_copy(gq_v, gq_hbm.at[0], o_sem.at[0])
    gq_copy.start()

    @pl.when(jnp.logical_not(is_home))
    def _():
        f_copy().wait_recv()

    gk_copy = pltpu.make_async_copy(gkv_v.at[pl.ds(0, 32)], gk_hbm.at[0], o_sem.at[1])
    gv_copy = pltpu.make_async_copy(gkv_v.at[pl.ds(32, 32)], gv_hbm.at[0], o_sem.at[2])
    gk_copy.start()
    gv_copy.start()

    @pl.when(is_home)
    def _():
        f_copy().wait_send()
        ag_copy(slot, 0, right).wait_send()
        ag_copy(slot, 1, left).wait_send()

    lax.fori_loop(1, 8, ag_drain, 0)

    def z_drain(at, carry):
        @pl.when(jnp.logical_not(jnp.logical_and(is_home, at == zpos)))
        def _():
            q_copy(at).wait_send()

        @pl.when(jnp.logical_not(jnp.logical_and(at % 2 == core, core * 8 + at // 2 == zpos)))
        def _():
            p1_copy(at).wait_send()

        return carry

    lax.fori_loop(0, 16, z_drain, 0)
    for step in (1, 2, 3):
        bias_all(step).wait_send()
        ds_copy(step).wait_send()

    def rs_drain(step, carry):
        @pl.when(to_right(step) // 8 == core)
        def _():
            rs_plus(step).wait_send()

        @pl.when(jnp.logical_and(step < 7, to_left(step) // 8 == core))
        def _():
            rs_minus(step).wait_send()

        return carry

    lax.fori_loop(0, 8, rs_drain, 0)

    def last_drain(step, carry):
        p2_copy(step).wait_send()
        return carry

    lax.fori_loop(1, 8, last_drain, 0)

    def gp_drain(pair, carry):
        gp_copy(pair).wait()
        return carry

    lax.fori_loop(0, 8, gp_drain, 0)
    gq_copy.wait()
    gk_copy.wait()
    gv_copy.wait()


def per_device(
    pair_feats, bucket_ids, ln_gain, w_in, b_in, w_out, bucket_table, key_mask,
    q_heads, k_heads, v_heads, out_heads, dout_heads, log_norm,
):
    any_space = pl.BlockSpec(memory_space=pl.ANY)
    vmem = pltpu.VMEM
    dma = pltpu.SemaphoreType.DMA
    return pl.pallas_call(
        kernel,
        out_shape=(
            jax.ShapeDtypeStruct((16, 64, 1024), BF16),
            jax.ShapeDtypeStruct((1, 32, 512), BF16),
            jax.ShapeDtypeStruct((1, 32, 1024), BF16),
            jax.ShapeDtypeStruct((1, 32, 1024), BF16),
        ),
        in_specs=[any_space] * 14,
        out_specs=(any_space,) * 4,
        scratch_shapes=[
            vmem((16, 64, 1024), BF16),
            vmem((16, 1024), jnp.int32),
            vmem((1, 64), F32),
            vmem((64, 256), BF16),
            vmem((1, 256), F32),
            vmem((32, 256), BF16),
            vmem((32, 32), BF16),
            vmem((1, 1024), jnp.int32),
            vmem((1, 32, 512), BF16),
            vmem((1, 32, 512), BF16),
            vmem((1, 32, 512), BF16),
            vmem((1, 512), F32),
            vmem((16, 64, 1024), BF16),
            vmem((32, 512), BF16),
            vmem((64, 1024), BF16),
            vmem((16, 256, 1024), BF16),
            vmem((16, 2, 1024), F32),
            vmem((8, 64, 1024), BF16),
            vmem((4, 8, 16, 1024), BF16),
            vmem((4, 8, 16, 1024), BF16),
            vmem((4, 128, 1024), BF16),
            vmem((4, 128, 1024), BF16),
            vmem((512, 1024), BF16),
            vmem((16, 32, 128), BF16),
            vmem((16, 32, 128), BF16),
            vmem((512, 256), BF16),
            vmem((512, 256), BF16),
            vmem((512, 128), F32),
            vmem((512, 128), F32),
            vmem((8, 64, 1024), F32),
            vmem((8, 64, 1024), BF16),
            vmem((8, 64, 1024), BF16),
            vmem((7, 64, 1024), BF16),
            vmem((7, 64, 1024), BF16),
            vmem((16, 8, 128), F32),
            vmem((16, 8, 128), F32),
            vmem((8, 16, 8, 128), F32),
            vmem((512, 128), BF16),
            vmem((512, 64), BF16),
            vmem((32, 256), BF16),
            vmem((32, 32), BF16),
            dma((11,)), dma((8,)), dma((2,)), dma((8,)), dma((3,)),
            dma((2, 8)), dma((8,)), dma((16,)), dma((16,)), dma((4,)), dma((4,)), dma((4,)), dma((4,)),
            dma((8,)), dma((8,)), dma((7,)), dma((7,)), dma, dma,
            dma((16,)), dma((16,)), dma((8,)), dma((8,)),
        ],
        compiler_params=pltpu.CompilerParams(
            collective_id=0, has_side_effects=True, vmem_limit_bytes=56 * 2**20
        ),
        name="pair_attention_backward",
    )(
        pair_feats, bucket_ids, ln_gain.reshape(1, 64), w_in, b_in.reshape(1, 256), w_out.T,
        bucket_table, key_mask.reshape(1, 1024), q_heads, k_heads, v_heads, out_heads, dout_heads, log_norm,
    )


def solution(mesh):
    return jax.shard_map(
        per_device,
        mesh=mesh,
        in_specs=(
            P(("query", "heads"), None, "key"),
            P(("query", "heads"), "key"),
            P(),
            P(),
            P(),
            P(),
            P(),
            P("key"),
            P("heads", None, "query"),
            P("heads", None, "key"),
            P("heads", None, "key"),
            P("heads", None, "query"),
            P("heads", None, "query"),
            P("heads", "query"),
        ),
        out_specs=(
            P(("query", "heads"), None, "key"),
            P("heads", None, "query"),
            P("heads", None, "key"),
            P("heads", None, "key"),
        ),
        check_vma=False,
    )
```

time: 330 us -> 104 us (0.32)
  the two profiles are of different devices: /device:TPU:1 before, /device:TPU:5 now
where the time goes in v1:
time: 104 us
  Pallas kernels  98.5 us (95%)
  local copies, waits for them, and re-layouts  5.06 us (5%)
    pallas_call x1, Pallas kernels, per_device(): pl.pallas_call(kernel, out_shape=(jax.ShapeDtypeStruct((16, 64, 1024), BF...  98.5 us
    unnamed x10, local copies, waits for them, and re-layouts  5.06 us

profile of v1, /device:TPU:5, one launch (start us, length us, event | category | flops | bytes accessed | tf_op | source)
XLA Modules:
  0.0 104.2 jit_solution(13111009287369087031)
XLA Ops:
  0.6 98.5 %pair_attention_backward.1 = (bf16[16,64,1024]{2,1,0:T(8,128)(2,1)}, bf16[1,32,512]{2,1,0:T(8,128)(2,1)}, bf16[1,32,1024]{2,1,0:T(8,128)(2,1)}, bf16[1,32,1024]{2,1,0:T(8,128)(2,1)}) custom-call(bf16[16,64,1024]{2,1,0:T(8,128)(2,1)} %x_hbm.1, s32[16,1024]{1,0:T(8,128)} %bucket_hbm.1, f32[1,64]{1,0:T(1,128)} %bitcast.7, bf16[64,256]{1,0:T(8,128)(2,1)} %win_hbm.1, ...), custom_call_target="tpu_custom_call" | custom-call | tf_op jit(solution)/shard_map/pair_attention_backward/pallas_call | solution.py:623
  99.2 0.0 copy-start.2
  99.2 0.0 copy-start.1
  99.2 0.0 copy-start
  99.2 3.2 %copy.22 = bf16[16,64,1024]{2,1,0:T(8,128)(2,1)} copy(bf16[16,64,1024]{2,1,0:T(8,128)(2,1)} %get-tuple-element.8) | data formatting | bytes 4194304
  102.4 0.0 copy-done.2
  102.4 0.6 copy.23
  103.0 0.0 copy-done.1
  103.0 0.6 copy.24
  103.6 0.0 copy-done
  103.6 0.6 copy.25
Async XLA Ops:
  99.2 3.2 %copy-start.2 = (bf16[1,32,512]{2,1,0:T(8,128)(2,1)S(1)}, bf16[1,32,512]{2,1,0:T(8,128)(2,1)}, u32[]{:S(2)}) copy-start(bf16[1,32,512]{2,1,0:T(8,128)(2,1)} %get-tuple-element.9) | copy-start | bytes 98308
  99.2 3.8 %copy-start.1 = (bf16[1,32,1024]{2,1,0:T(8,128)(2,1)S(1)}, bf16[1,32,1024]{2,1,0:T(8,128)(2,1)}, u32[]{:S(2)}) copy-start(bf16[1,32,1024]{2,1,0:T(8,128)(2,1)} %get-tuple-element.10) | copy-start | bytes 196612
  99.2 4.4 %copy-start = (bf16[1,32,1024]{2,1,0:T(8,128)(2,1)S(1)}, bf16[1,32,1024]{2,1,0:T(8,128)(2,1)}, u32[]{:S(2)}) copy-start(bf16[1,32,1024]{2,1,0:T(8,128)(2,1)} %get-tuple-element.11) | copy-start | bytes 196612

commit v2 on v1

--- a/solution.py
+++ b/solution.py
@@ -51,14 +51,14 @@
     x_v, bucket_v, gain_v, win_v, bin_v, woutt_v, table_v, mask_v,
     q_v, out_v, dout_v, norm_v,
     gp_v, gq_v, gkv_v,
-    slope_v, stat_v, kv_v, bias_out, bias_in, ds_all, ds_in, probs_v,
+    slope_v, stat_v, kv_v, bias_out, bias_in, ds_all, ds_in, probs_v, probs_f,
     qstage, qrecv, qblk_v, doblk_v, norm_b, delta_b, dkv_v,
     rsp_send, rsp_recv, rsm_send, rsm_recv,
     dq_send, dq_recv, dq_peers, w1_v, w2_v, wmix_v, tab_v,
     in_sem, x_sem, kv_sem, gp_sem, o_sem,
     ag_send, ag_recv, q_send, q_recv, b_send, b_recv, d_send, d_recv,
     rp_send, rp_recv, rm_send, rm_recv, f_send, f_recv,
-    p1_send, p1_recv, p2_send, p2_recv,
+    p1_send, p1_recv, p2_send, p2_recv, round_one, round_two,
 ):
     core = lax.axis_index("query")
     key = lax.axis_index("key")
@@ -74,8 +74,13 @@
     def device(core_at, z_at, y_at):
         return (core_at, key, z_at * 2 + y_at)
 
-    right = device(core, (zpos + 1) % 16, ypos)
-    left = device(core, (zpos + 15) % 16, ypos)
+    def along(hops):
+        return device(core, (zpos + 16 + hops) % 16, ypos)
+
+    def along_x(hops):
+        return (core, (key + 8 + 2 * hops) % 8, col)
+
+    across_y = (core, key + 1 - 2 * (key % 2), col)
 
     def quad(step):
         core_at = (core + step // 2) % 2
@@ -87,29 +92,14 @@
     def greet(where):
         pl.semaphore_signal(barrier, inc=1, device_id=where, device_id_type=MESH)
 
-    greet(right)
-    greet(left)
+    for hops in (1, -1, 2, -2):
+        greet(along(hops))
+        greet(device(1 - core, (zpos + 16 + hops) % 16, ypos))
     for step in (1, 2, 3):
         greet(quad(step)[0])
-
-    def greet_z(at, carry):
-        @pl.when(jnp.logical_not(jnp.logical_and(is_home, at == zpos)))
-        def _():
-            greet(device(home, at, ypos))
-
-        @pl.when(jnp.logical_not(jnp.logical_and(core == at // 8, core * 8 + at % 8 == zpos)))
-        def _():
-            greet(device(at // 8, core * 8 + at % 8, ypos))
-
-        return carry
-
-    lax.fori_loop(0, 16, greet_z, 0)
-
-    def greet_key(step, carry):
-        greet((core, (key + step) % 8, col))
-        return carry
-
-    lax.fori_loop(1, 8, greet_key, 0)
+    greet(along_x(1))
+    greet(along_x(-1))
+    greet(across_y)
 
     loads = [
         pltpu.make_async_copy(src, dst, in_sem.at[at])
@@ -130,8 +120,8 @@
     for pair in range(8):
         x_load(pair).start()
 
-    k_load = pltpu.make_async_copy(k_hbm.at[0], kv_v.at[slot, pl.ds(0, 32)], kv_sem.at[0])
-    v_load = pltpu.make_async_copy(v_hbm.at[0], kv_v.at[slot, pl.ds(32, 32)], kv_sem.at[1])
+    k_load = pltpu.make_async_copy(k_hbm.at[0], kv_v.at[0, slot], kv_sem.at[0])
+    v_load = pltpu.make_async_copy(v_hbm.at[0], kv_v.at[1, slot], kv_sem.at[1])
 
     @pl.when(is_home)
     def _():
@@ -185,45 +175,38 @@
             recv_sem=q_recv.at[at], device_id=device(at % 2, core * 8 + at // 2, ypos), device_id_type=MESH,
         )
 
-    def ag_copy(at, way, where):
-        return pltpu.make_async_remote_copy(
-            src_ref=kv_v.at[at], dst_ref=kv_v.at[at], send_sem=ag_send.at[way, at],
-            recv_sem=ag_recv.at[at], device_id=where, device_id_type=MESH,
-        )
-
-    def ag_step(step):
-        from_left = (zpos + 16 - step) % 16
-        from_right = (zpos + step) % 16
-
-        @pl.when(jnp.logical_and(step <= 8, from_left // 8 == core))
-        def _():
-            ag_copy(from_left % 8, 0, right).wait_recv()
-
-            @pl.when(step < 8)
+    def ag_copy(half, at, way, hops):
+        return pltpu.make_async_remote_copy(
+            src_ref=kv_v.at[half, at], dst_ref=kv_v.at[half, at],
+            send_sem=ag_send.at[half, way * 2 + hops - 1, at],
+            recv_sem=ag_recv.at[half, at], device_id=along(hops - 2 * hops * way), device_id_type=MESH,
+        )
+
+    def ag_source(way, hops):
+        return (zpos + 16 - hops + 2 * hops * way) % 16
+
+    def ag_forward(half, hops, ending=False):
+        for way in range(2):
+            source = ag_source(way, hops)
+
+            @pl.when(source // 8 == core)
             def _():
-                ag_copy(from_left % 8, 0, right).start()
-
-        @pl.when(jnp.logical_and(step <= 7, from_right // 8 == core))
-        def _():
-            ag_copy(from_right % 8, 1, left).wait_recv()
-
-            @pl.when(step < 7)
+                onward = [ag_copy(half, source % 8, way, hop) for hop in ((1,) if way == 1 and hops == 6 else (2, 1))]
+                if ending:
+                    for copy in onward:
+                        copy.wait_send()
+                else:
+                    onward[0].wait_recv()
+                    for copy in onward:
+                        copy.start()
+
+    def ag_finish(half):
+        for way, hops in ((0, 1), (0, 3), (0, 5), (0, 7), (0, 8), (1, 1), (1, 3), (1, 5), (1, 7)):
+            source = ag_source(way, hops)
+
+            @pl.when(source // 8 == core)
             def _():
-                ag_copy(from_right % 8, 1, left).start()
-
-    def ag_drain(step, carry):
-        from_left = (zpos + 16 - step) % 16
-        from_right = (zpos + step) % 16
-
-        @pl.when(jnp.logical_and(step < 8, from_left // 8 == core))
-        def _():
-            ag_copy(from_left % 8, 0, right).wait_send()
-
-        @pl.when(jnp.logical_and(step < 7, from_right // 8 == core))
-        def _():
-            ag_copy(from_right % 8, 1, left).wait_send()
-
-        return carry
+                ag_copy(half, source % 8, way, 1).wait_recv()
 
     def bias_copy(step, pair):
         where, part = quad(step)
@@ -262,23 +245,30 @@
             rows = [mix[part * 8:(part + 1) * 8] for mix in mixes]
             bias_out[part, pair] = jnp.concatenate(rows, axis=0).astype(BF16)
 
-    forward_pair(0)
-
-    @pl.when(is_home)
-    def _():
-        pl.semaphore_wait(barrier, 42)
-
-    @pl.when(jnp.logical_not(is_home))
-    def _():
-        pl.semaphore_wait(barrier, 44)
+    def bias_send(pair):
+        for step in (1, 2, 3):
+            bias_copy(step, pair).start()
+
+    def forward_only(pair, carry):
+        forward_pair(pair)
+        return carry
+
+    lax.fori_loop(0, 2, forward_only, 0)
+    pl.semaphore_wait(barrier, 14)
 
     @pl.when(is_home)
     def _():
         k_load.wait()
         v_load.wait()
-        ag_copy(slot, 0, right).start()
-        ag_copy(slot, 1, left).start()
-        qrecv[slot * 2 + core] = qstage[zpos]
+        for half in range(2):
+            for hops in (2, 1):
+                ag_copy(half, slot, 0, hops).start()
+                ag_copy(half, slot, 1, hops).start()
+
+    for where in (along(2), along(-2), along_x(1), along_x(-1)):
+        pl.semaphore_signal(round_one, inc=1, device_id=where, device_id_type=MESH)
+    bias_send(0)
+    bias_send(1)
 
     def q_start(at, carry):
         @pl.when(jnp.logical_not(jnp.logical_and(is_home, at == zpos)))
@@ -287,18 +277,40 @@
 
         return carry
 
-    lax.fori_loop(0, 16, q_start, 0)
-    for step in (1, 2, 3):
-        bias_copy(step, 0).start()
-
     def forward_body(pair, carry):
         forward_pair(pair)
-        for step in (1, 2, 3):
-            bias_copy(step, pair).start()
-        ag_step(pair)
-        return carry
-
-    lax.fori_loop(1, 8, forward_body, 0)
+        bias_send(pair)
+
+        @pl.when(pair == 3)
+        def _():
+            pl.semaphore_wait(round_one, 4)
+            for where in (along(4), along(-4), across_y):
+                pl.semaphore_signal(round_two, inc=1, device_id=where, device_id_type=MESH)
+            ag_forward(0, 2)
+
+        @pl.when(pair == 4)
+        def _():
+            ag_forward(1, 2)
+
+        @pl.when(pair == 5)
+        def _():
+            pl.semaphore_wait(round_two, 3)
+            lax.fori_loop(0, 16, q_start, 0)
+            ag_forward(0, 4)
+
+        @pl.when(pair == 6)
+        def _():
+            ag_forward(1, 4)
+
+        return carry
+
+    lax.fori_loop(2, 8, forward_body, 0)
+
+    @pl.when(is_home)
+    def _():
+        qrecv[slot * 2 + core] = qstage[zpos]
+
+    ag_forward(0, 6)
 
     def q_wait(at, carry):
         @pl.when(jnp.logical_not(jnp.logical_and(at % 2 == core, core * 8 + at // 2 == zpos)))
@@ -320,24 +332,10 @@
     norm_b[...] = dot(by_row, ones_where(jnp.logical_and(wide >= 64, wide < 67)))
     delta_b[...] = dot(by_row, ones_where(jnp.logical_and(wide >= 67, wide < 70)))
 
-    ag_step(8)
+    ag_forward(1, 6)
     live = mask_v[...] == 1
-    keys = kv_v[:, 0:32, :].reshape(256, 1024)
-    values = kv_v[:, 32:64, :].reshape(256, 1024)
-
-    def ds_copy(step):
-        where, part = quad(step)
-        return pltpu.make_async_remote_copy(
-            src_ref=ds_all.at[part], dst_ref=ds_in.at[mine], send_sem=d_send.at[step],
-            recv_sem=d_recv.at[mine], device_id=where, device_id_type=MESH,
-        )
-
-    def ds_arrival(step):
-        where, part = quad(step)
-        return pltpu.make_async_remote_copy(
-            src_ref=ds_all.at[part], dst_ref=ds_in.at[part], send_sem=d_send.at[step],
-            recv_sem=d_recv.at[part], device_id=where, device_id_type=MESH,
-        )
+    ag_finish(0)
+    keys = kv_v[0].reshape(256, 1024)
 
     for step in (1, 2, 3, 0):
         _, part = quad(step)
@@ -350,59 +348,83 @@
         scores = dot(qblk_v[rows, :], keys) * score_scale + bias.reshape(128, 1024).astype(F32)
         shift = jnp.concatenate([norm_b[rows, :]] * 8, axis=1)
         probs = jnp.where(live, jnp.exp(scores - shift), 0.0)
+        probs_f[rows, :] = probs
         probs_v[rows, :] = probs.astype(BF16)
+    dkv_v[:, 32:64, :] = dot(doblk_v[...].T, probs_v[...]).reshape(8, 32, 1024)
+
+    def rs_copy(way, far, half):
+        hops = 2 if far == 8 or far % 2 == 0 else 1
+        send, recv, s_sem, r_sem = (
+            (rsp_send, rsp_recv, rp_send, rp_recv), (rsm_send, rsm_recv, rm_send, rm_recv)
+        )[way]
+        return pltpu.make_async_remote_copy(
+            src_ref=send.at[far - 1, half], dst_ref=recv.at[far - 1, half], send_sem=s_sem.at[far - 1, half],
+            recv_sem=r_sem.at[far - 1, half], device_id=along(-hops if way else hops), device_id_type=MESH,
+        )
+
+    def rs_dest(way, far):
+        return (zpos + 16 - far if way else zpos + far) % 16
+
+    def rs_part(far, half, way):
+        dest = rs_dest(way, far)
+        send, recv = ((rsp_send, rsp_recv), (rsm_send, rsm_recv))[way]
+        last = 7 if way else 8
+
+        @pl.when(dest // 8 == core)
+        def _():
+            total = dkv_v[dest % 8, half * 32:half * 32 + 32, :]
+            if far in (2, 4, 6):
+                for other in (far + 1, far + 2):
+                    if other <= last:
+                        rs_copy(way, other, half).wait_recv()
+                        total = total + recv[other - 1, half].astype(F32)
+            send[far - 1, half] = total.astype(BF16)
+            rs_copy(way, far, half).start()
+
+    def rs_raw(half):
+        for far in (8, 7, 5, 3, 1):
+            for way in range(2):
+                if not (way == 1 and far == 8):
+                    rs_part(far, half, way)
+
+    def rs_sum(far, half):
+        for way in range(2):
+            rs_part(far, half, way)
+
+    rs_raw(1)
+    ag_finish(1)
+    values = kv_v[1].reshape(256, 1024)
+
+    def ds_copy(step, piece):
+        where, part = quad(step)
+        at = pl.ds(piece * 32, 32)
+        return pltpu.make_async_remote_copy(
+            src_ref=ds_all.at[part, at], dst_ref=ds_in.at[mine, at], send_sem=d_send.at[step, piece],
+            recv_sem=d_recv.at[mine, piece], device_id=where, device_id_type=MESH,
+        )
+
+    def ds_arrival(step, piece):
+        where, part = quad(step)
+        at = pl.ds(pl.multiple_of(piece * 32, 32), 32)
+        return pltpu.make_async_remote_copy(
+            src_ref=ds_all.at[part, at], dst_ref=ds_in.at[part, at], send_sem=d_send.at[step, piece],
+            recv_sem=d_recv.at[part, piece], device_id=where, device_id_type=MESH,
+        )
+
+    for step in (1, 3, 2, 0):
+        _, part = quad(step)
+        rows = pl.ds(pl.multiple_of(part * 128, 128), 128)
         less = jnp.concatenate([delta_b[rows, :]] * 8, axis=1)
-        dscores = (probs * (dot(doblk_v[rows, :], values) - less)).astype(BF16)
+        dscores = (probs_f[rows, :] * (dot(doblk_v[rows, :], values) - less)).astype(BF16)
         ds_all[part] = dscores
-        if step:
-            ds_copy(step).start()
-        else:
+        if not step:
             ds_in[part] = dscores
-
+    for piece in range(4):
+        for step in (1, 3, 2):
+            ds_copy(step, piece).start()
     ds_flat = ds_all[...].reshape(512, 1024)
     dkv_v[:, 0:32, :] = dot(qblk_v[...].T, ds_flat).reshape(8, 32, 1024)
-    dkv_v[:, 32:64, :] = dot(doblk_v[...].T, probs_v[...]).reshape(8, 32, 1024)
-
-    def rs_plus(step):
-        return pltpu.make_async_remote_copy(
-            src_ref=rsp_send.at[step], dst_ref=rsp_recv.at[step], send_sem=rp_send.at[step],
-            recv_sem=rp_recv.at[step], device_id=right, device_id_type=MESH,
-        )
-
-    def rs_minus(step):
-        return pltpu.make_async_remote_copy(
-            src_ref=rsm_send.at[step], dst_ref=rsm_recv.at[step], send_sem=rm_send.at[step],
-            recv_sem=rm_recv.at[step], device_id=left, device_id_type=MESH,
-        )
-
-    def to_right(step):
-        return (zpos + 8 - step) % 16
-
-    def to_left(step):
-        return (zpos + 9 + step) % 16
-
-    @pl.when(to_right(0) // 8 == core)
-    def _():
-        rsp_send[0] = dkv_v[to_right(0) % 8].astype(BF16)
-        rs_plus(0).start()
-
-    @pl.when(to_left(0) // 8 == core)
-    def _():
-        rsm_send[0] = dkv_v[to_left(0) % 8].astype(BF16)
-        rs_minus(0).start()
-
-    def rs_step(step):
-        @pl.when(jnp.logical_and(step < 8, to_right(step) // 8 == core))
-        def _():
-            rs_plus(step - 1).wait_recv()
-            rsp_send[step] = (rsp_recv[step - 1].astype(F32) + dkv_v[to_right(step) % 8]).astype(BF16)
-            rs_plus(step).start()
-
-        @pl.when(jnp.logical_and(step < 7, to_left(step) // 8 == core))
-        def _():
-            rs_minus(step - 1).wait_recv()
-            rsm_send[step] = (rsm_recv[step - 1].astype(F32) + dkv_v[to_left(step) % 8]).astype(BF16)
-            rs_minus(step).start()
+    rs_raw(0)
 
     dq_full = lax.dot_general(ds_flat, keys, (((1,), (1,)), ((), ())), preferred_element_type=F32)
     dq_full = jnp.where(own_head, dq_full, 0.0)
@@ -478,9 +500,6 @@
 
         lax.fori_loop(1, 8, p2_start, 0)
 
-    for step in (1, 2, 3):
-        ds_arrival(step).wait_recv()
-
     win = win_v[...]
 
     def gp_copy(pair):
@@ -501,17 +520,26 @@
         gp_copy(pair).start()
 
     def backward_body(pair, carry):
+        @pl.when(pair % 2 == 0)
+        def _():
+            for step in (1, 2, 3):
+                ds_arrival(step, pair // 2).wait_recv()
+
         backward_pair(pair)
-        rs_step(pair + 1)
-
-        @pl.when(pair == 3)
+        for at, (far, half) in ((1, (6, 1)), (2, (6, 0)), (4, (4, 1)), (6, (4, 0))):
+            @pl.when(pair == at)
+            def _():
+                rs_sum(far, half)
+
+        @pl.when(pair == 5)
         def _():
             phase_two()
 
         return carry
 
-    lax.fori_loop(0, 7, backward_body, 0)
-    backward_pair(7)
+    lax.fori_loop(0, 8, backward_body, 0)
+    rs_sum(2, 1)
+    rs_sum(2, 0)
 
     sibling, _ = quad(2)
 
@@ -523,9 +551,12 @@
 
     @pl.when(is_home)
     def _():
-        rs_plus(7).wait_recv()
-        rs_minus(6).wait_recv()
-        total = dkv_v[slot] + rsp_recv[7].astype(F32) + rsm_recv[6].astype(F32)
+        total = dkv_v[slot]
+        for way, recv in ((0, rsp_recv), (1, rsm_recv)):
+            for far in (1, 2):
+                for half in range(2):
+                    rs_copy(way, far, half).wait_recv()
+                total = total + recv[far - 1].reshape(64, 1024).astype(F32)
         gkv_v[0:32, :] = (total[0:32] * score_scale).astype(BF16)
         gkv_v[32:64, :] = total[32:64].astype(BF16)
         f_copy().start()
@@ -563,10 +594,14 @@
     @pl.when(is_home)
     def _():
         f_copy().wait_send()
-        ag_copy(slot, 0, right).wait_send()
-        ag_copy(slot, 1, left).wait_send()
-
-    lax.fori_loop(1, 8, ag_drain, 0)
+        for half in range(2):
+            for hops in (2, 1):
+                ag_copy(half, slot, 0, hops).wait_send()
+                ag_copy(half, slot, 1, hops).wait_send()
+
+    for half in range(2):
+        for hops in (2, 4, 6):
+            ag_forward(half, hops, True)
 
     def z_drain(at, carry):
         @pl.when(jnp.logical_not(jnp.logical_and(is_home, at == zpos)))
@@ -582,20 +617,15 @@
     lax.fori_loop(0, 16, z_drain, 0)
     for step in (1, 2, 3):
         bias_all(step).wait_send()
-        ds_copy(step).wait_send()
-
-    def rs_drain(step, carry):
-        @pl.when(to_right(step) // 8 == core)
-        def _():
-            rs_plus(step).wait_send()
-
-        @pl.when(jnp.logical_and(step < 7, to_left(step) // 8 == core))
-        def _():
-            rs_minus(step).wait_send()
-
-        return carry
-
-    lax.fori_loop(0, 8, rs_drain, 0)
+        for piece in range(4):
+            ds_copy(step, piece).wait_send()
+
+    for half in range(2):
+        for way, last in ((0, 8), (1, 7)):
+            for far in range(1, last + 1):
+                @pl.when(rs_dest(way, far) // 8 == core)
+                def _():
+                    rs_copy(way, far, half).wait_send()
 
     def last_drain(step, carry):
         p2_copy(step).wait_send()
@@ -611,6 +641,16 @@
     gq_copy.wait()
     gk_copy.wait()
     gv_copy.wait()
+
+
+def hand_over(gp_in, gq_in, gk_in, gv_in, gp_out, gq_out, gk_out, gv_out, row_sem, small_sem):
+    copies = [pltpu.make_async_copy(gp_in.at[row], gp_out.at[row], row_sem.at[row]) for row in range(16)]
+    for at, (src, dst) in enumerate(((gq_in, gq_out), (gk_in, gk_out), (gv_in, gv_out))):
+        copies.append(pltpu.make_async_copy(src, dst, small_sem.at[at]))
+    for copy in copies:
+        copy.start()
+    for copy in copies:
+        copy.wait()
 
 
 def per_device(
@@ -620,7 +660,7 @@
     any_space = pl.BlockSpec(memory_space=pl.ANY)
     vmem = pltpu.VMEM
     dma = pltpu.SemaphoreType.DMA
-    return pl.pallas_call(
+    results = pl.pallas_call(
         kernel,
         out_shape=(
             jax.ShapeDtypeStruct((16, 64, 1024), BF16),
@@ -648,12 +688,13 @@
             vmem((64, 1024), BF16),
             vmem((16, 256, 1024), BF16),
             vmem((16, 2, 1024), F32),
-            vmem((8, 64, 1024), BF16),
+            vmem((2, 8, 32, 1024), BF16),
             vmem((4, 8, 16, 1024), BF16),
             vmem((4, 8, 16, 1024), BF16),
             vmem((4, 128, 1024), BF16),
             vmem((4, 128, 1024), BF16),
             vmem((512, 1024), BF16),
+            vmem((512, 1024), F32),
             vmem((16, 32, 128), BF16),
             vmem((16, 32, 128), BF16),
             vmem((512, 256), BF16),
@@ -661,10 +702,10 @@
             vmem((512, 128), F32),
             vmem((512, 128), F32),
             vmem((8, 64, 1024), F32),
-            vmem((8, 64, 1024), BF16),
-            vmem((8, 64, 1024), BF16),
-            vmem((7, 64, 1024), BF16),
-            vmem((7, 64, 1024), BF16),
+            vmem((8, 2, 32, 1024), BF16),
+            vmem((8, 2, 32, 1024), BF16),
+            vmem((7, 2, 32, 1024), BF16),
+            vmem((7, 2, 32, 1024), BF16),
             vmem((16, 8, 128), F32),
             vmem((16, 8, 128), F32),
             vmem((8, 16, 8, 128), F32),
@@ -673,9 +714,10 @@
             vmem((32, 256), BF16),
             vmem((32, 32), BF16),
             dma((11,)), dma((8,)), dma((2,)), dma((8,)), dma((3,)),
-            dma((2, 8)), dma((8,)), dma((16,)), dma((16,)), dma((4,)), dma((4,)), dma((4,)), dma((4,)),
-            dma((8,)), dma((8,)), dma((7,)), dma((7,)), dma, dma,
+            dma((2, 4, 8)), dma((2, 8)), dma((16,)), dma((16,)), dma((4,)), dma((4,)), dma((4, 4)), dma((4, 4)),
+            dma((8, 2)), dma((8, 2)), dma((7, 2)), dma((7, 2)), dma, dma,
             dma((16,)), dma((16,)), dma((8,)), dma((8,)),
+            pltpu.SemaphoreType.REGULAR, pltpu.SemaphoreType.REGULAR,
         ],
         compiler_params=pltpu.CompilerParams(
             collective_id=0, has_side_effects=True, vmem_limit_bytes=56 * 2**20
@@ -685,6 +727,14 @@
         pair_feats, bucket_ids, ln_gain.reshape(1, 64), w_in, b_in.reshape(1, 256), w_out.T,
         bucket_table, key_mask.reshape(1, 1024), q_heads, k_heads, v_heads, out_heads, dout_heads, log_norm,
     )
+    return pl.pallas_call(
+        hand_over,
+        out_shape=tuple(jax.ShapeDtypeStruct(member.shape, member.dtype) for member in results),
+        in_specs=[any_space] * 4,
+        out_specs=(any_space,) * 4,
+        scratch_shapes=[dma((16,)), dma((3,))],
+        name="hand_over",
+    )(*results)
 
 
 def solution(mesh):

time: 104 us -> 141 us (1.36)
  the two profiles are of different devices: /device:TPU:5 before, /device:TPU:1 now
where the time goes in v2:
time: 141 us
  Pallas kernels  141 us (100%)
    pallas_call x1, Pallas kernels, per_device(): pl.pallas_call(kernel, out_shape=(jax.ShapeDtypeStruct((16, 64, 1024), BF...  70.9 us
    pallas_call x1, Pallas kernels, per_device(): pl.pallas_call(hand_over, out_shape=tuple((jax.ShapeDtypeStruct(member.sh...  69.8 us

profile of v2, /device:TPU:1, one launch (start us, length us, event | category | flops | bytes accessed | tf_op | source)
XLA Modules:
  0.0 141.3 jit_solution(3354060719323613676)
XLA Ops:
  0.6 70.9 %pair_attention_backward.1 = (bf16[16,64,1024]{2,1,0:T(8,128)(2,1)}, bf16[1,32,512]{2,1,0:T(8,128)(2,1)}, bf16[1,32,1024]{2,1,0:T(8,128)(2,1)}, bf16[1,32,1024]{2,1,0:T(8,128)(2,1)}) custom-call(bf16[16,64,1024]{2,1,0:T(8,128)(2,1)} %x_hbm.1, s32[16,1024]{1,0:T(8,128)} %bucket_hbm.1, f32[1,64]{1,0:T(1,128)} %bitcast.7, bf16[64,256]{1,0:T(8,128)(2,1)} %win_hbm.1, ...), custom_call_target="tpu_custom_call" | custom-call | tf_op jit(solution)/shard_map/pair_attention_backward/pallas_call | solution.py:663
  71.5 69.8 %hand_over.1 = (bf16[16,64,1024]{2,1,0:T(8,128)(2,1)}, bf16[1,32,512]{2,1,0:T(8,128)(2,1)}, bf16[1,32,1024]{2,1,0:T(8,128)(2,1)}, bf16[1,32,1024]{2,1,0:T(8,128)(2,1)}) custom-call(bf16[16,64,1024]{2,1,0:T(8,128)(2,1)} %get-tuple-element.8.gp_in, bf16[1,32,512]{2,1,0:T(8,128)(2,1)} %get-tuple-element.9.gq_in, bf16[1,32,1024]{2,1,0:T(8,128)(2,1)} %get-tuple-element.10.gk_in, ...), custom_call_target="tpu_custom_call" | custom-call | tf_op jit(solution)/shard_map/hand_over/pallas_call | solution.py:730

commit v3 on v2

--- a/solution.py
+++ b/solution.py
@@ -249,11 +249,6 @@
         for step in (1, 2, 3):
             bias_copy(step, pair).start()
 
-    def forward_only(pair, carry):
-        forward_pair(pair)
-        return carry
-
-    lax.fori_loop(0, 2, forward_only, 0)
     pl.semaphore_wait(barrier, 14)
 
     @pl.when(is_home)
@@ -267,8 +262,6 @@
 
     for where in (along(2), along(-2), along_x(1), along_x(-1)):
         pl.semaphore_signal(round_one, inc=1, device_id=where, device_id_type=MESH)
-    bias_send(0)
-    bias_send(1)
 
     def q_start(at, carry):
         @pl.when(jnp.logical_not(jnp.logical_and(is_home, at == zpos)))
@@ -281,22 +274,22 @@
         forward_pair(pair)
         bias_send(pair)
 
-        @pl.when(pair == 3)
+        @pl.when(pair == 2)
         def _():
             pl.semaphore_wait(round_one, 4)
             for where in (along(4), along(-4), across_y):
                 pl.semaphore_signal(round_two, inc=1, device_id=where, device_id_type=MESH)
             ag_forward(0, 2)
 
-        @pl.when(pair == 4)
+        @pl.when(pair == 3)
         def _():
             ag_forward(1, 2)
 
         @pl.when(pair == 5)
         def _():
+            ag_forward(0, 4)
             pl.semaphore_wait(round_two, 3)
             lax.fori_loop(0, 16, q_start, 0)
-            ag_forward(0, 4)
 
         @pl.when(pair == 6)
         def _():
@@ -304,7 +297,7 @@
 
         return carry
 
-    lax.fori_loop(2, 8, forward_body, 0)
+    lax.fori_loop(0, 8, forward_body, 0)
 
     @pl.when(is_home)
     def _():
@@ -423,9 +416,6 @@
         for step in (1, 3, 2):
             ds_copy(step, piece).start()
     ds_flat = ds_all[...].reshape(512, 1024)
-    dkv_v[:, 0:32, :] = dot(qblk_v[...].T, ds_flat).reshape(8, 32, 1024)
-    rs_raw(0)
-
     dq_full = lax.dot_general(ds_flat, keys, (((1,), (1,)), ((), ())), preferred_element_type=F32)
     dq_full = jnp.where(own_head, dq_full, 0.0)
     dq_fold = dq_full[:, 0:128] + dq_full[:, 128:256]
@@ -470,16 +460,20 @@
     def _():
         dq_recv[zpos] = dq_send[slot * 2 + core]
 
+    dkv_v[:, 0:32, :] = dot(qblk_v[...].T, ds_flat).reshape(8, 32, 1024)
+    rs_raw(0)
+    rs_sum(6, 1)
+
     def p2_copy(step):
         return pltpu.make_async_remote_copy(
-            src_ref=dq_recv, dst_ref=dq_peers.at[key], send_sem=p2_send.at[step],
+            src_ref=dq_peers.at[key], dst_ref=dq_peers.at[key], send_sem=p2_send.at[step],
             recv_sem=p2_recv.at[key], device_id=(core, (key + step) % 8, col), device_id_type=MESH,
         )
 
     def p2_arrival(step):
         peer = (key + step) % 8
         return pltpu.make_async_remote_copy(
-            src_ref=dq_recv, dst_ref=dq_peers.at[peer], send_sem=p2_send.at[step],
+            src_ref=dq_peers.at[key], dst_ref=dq_peers.at[peer], send_sem=p2_send.at[step],
             recv_sem=p2_recv.at[peer], device_id=(core, peer, col), device_id_type=MESH,
         )
 
@@ -492,7 +486,7 @@
             return carry
 
         lax.fori_loop(0, 16, p1_wait, 0)
-        dq_peers[key] = dq_recv[...]
+        dq_peers[key] = dq_recv[...].reshape(128, 128).astype(BF16)
 
         def p2_start(step, carry):
             p2_copy(step).start()
@@ -526,7 +520,7 @@
                 ds_arrival(step, pair // 2).wait_recv()
 
         backward_pair(pair)
-        for at, (far, half) in ((1, (6, 1)), (2, (6, 0)), (4, (4, 1)), (6, (4, 0))):
+        for at, (far, half) in ((1, (6, 0)), (2, (4, 1)), (4, (4, 0)), (6, (2, 1))):
             @pl.when(pair == at)
             def _():
                 rs_sum(far, half)
@@ -538,7 +532,6 @@
         return carry
 
     lax.fori_loop(0, 8, backward_body, 0)
-    rs_sum(2, 1)
     rs_sum(2, 0)
 
     sibling, _ = quad(2)
@@ -566,10 +559,10 @@
         return carry
 
     lax.fori_loop(1, 8, p2_wait, 0)
-    total_q = dq_peers[0]
+    total_q = dq_peers[0].astype(F32)
     for at in range(1, 8):
-        total_q = total_q + dq_peers[at]
-    final_q = (total_q.reshape(128, 128) * score_scale).astype(BF16).astype(F32).T.astype(BF16)
+        total_q = total_q + dq_peers[at].astype(F32)
+    final_q = (total_q * score_scale).astype(BF16).astype(F32).T.astype(BF16)
     lane_a, lane_b = iota((128, 512), 0), iota((128, 512), 1)
     grad_q = jnp.zeros((32, 512), F32)
     for at in range(4):
@@ -643,14 +636,20 @@
     gv_copy.wait()
 
 
-def hand_over(gp_in, gq_in, gk_in, gv_in, gp_out, gq_out, gk_out, gv_out, row_sem, small_sem):
-    copies = [pltpu.make_async_copy(gp_in.at[row], gp_out.at[row], row_sem.at[row]) for row in range(16)]
-    for at, (src, dst) in enumerate(((gq_in, gq_out), (gk_in, gk_out), (gv_in, gv_out))):
-        copies.append(pltpu.make_async_copy(src, dst, small_sem.at[at]))
-    for copy in copies:
-        copy.start()
-    for copy in copies:
-        copy.wait()
+def hand_over(gp_in, gq_in, gk_in, gv_in, gp_out, gq_out, gk_out, gv_out, gp_v, gq_v, gk_v, gv_v, in_sem, out_sem):
+    stages = [(gq_in, gq_v, gq_out), (gk_in, gk_v, gk_out), (gv_in, gv_v, gv_out)]
+    for at in range(8):
+        rows = pl.ds(at * 2, 2)
+        stages.append((gp_in.at[rows], gp_v.at[rows], gp_out.at[rows]))
+    loads = [pltpu.make_async_copy(src, mid, in_sem.at[at]) for at, (src, mid, _) in enumerate(stages)]
+    stores = [pltpu.make_async_copy(mid, dst, out_sem.at[at]) for at, (_, mid, dst) in enumerate(stages)]
+    for load in loads:
+        load.start()
+    for load, store in zip(loads, stores):
+        load.wait()
+        store.start()
+    for store in stores:
+        store.wait()
 
 
 def per_device(
@@ -708,7 +707,7 @@
             vmem((7, 2, 32, 1024), BF16),
             vmem((16, 8, 128), F32),
             vmem((16, 8, 128), F32),
-            vmem((8, 16, 8, 128), F32),
+            vmem((8, 128, 128), BF16),
             vmem((512, 128), BF16),
             vmem((512, 64), BF16),
             vmem((32, 256), BF16),
@@ -732,7 +731,10 @@
         out_shape=tuple(jax.ShapeDtypeStruct(member.shape, member.dtype) for member in results),
         in_specs=[any_space] * 4,
         out_specs=(any_space,) * 4,
-        scratch_shapes=[dma((16,)), dma((3,))],
+        scratch_shapes=[
+            vmem((16, 64, 1024), BF16), vmem((1, 32, 512), BF16), vmem((1, 32, 1024), BF16), vmem((1, 32, 1024), BF16),
+            dma((11,)), dma((11,)),
+        ],
         name="hand_over",
     )(*results)
 

time: 141 us -> 74.3 us (0.53)
  Pallas kernels: 141 us -> 72.7 us
    pallas_call x1, Pallas kernels: 69.8 us -> 2.54 us  [per_device(): pl.pallas_call(hand_over, out_shape=tuple((jax.ShapeDtypeStruct(member.sh...]
where the time goes in v3:
time: 74.3 us; the launch traced here: 73.4 us
  Pallas kernels  72.7 us (98%)
    pallas_call x1, Pallas kernels, per_device(): pl.pallas_call(kernel, out_shape=(jax.ShapeDtypeStruct((16, 64, 1024), BF...  70.2 us
    pallas_call x1, Pallas kernels, per_device(): pl.pallas_call(hand_over, out_shape=tuple((jax.ShapeDtypeStruct(member.sh...  2.54 us

profile of v3, /device:TPU:1, one launch (start us, length us, event | category | flops | bytes accessed | tf_op | source)
XLA Modules:
  0.0 73.4 jit_solution(2906141874444636198)
XLA Ops:
  0.6 70.2 %pair_attention_backward.1 = (bf16[16,64,1024]{2,1,0:T(8,128)(2,1)}, bf16[1,32,512]{2,1,0:T(8,128)(2,1)}, bf16[1,32,1024]{2,1,0:T(8,128)(2,1)}, bf16[1,32,1024]{2,1,0:T(8,128)(2,1)}) custom-call(bf16[16,64,1024]{2,1,0:T(8,128)(2,1)} %x_hbm.1, s32[16,1024]{1,0:T(8,128)} %bucket_hbm.1, f32[1,64]{1,0:T(1,128)} %bitcast.7, bf16[64,256]{1,0:T(8,128)(2,1)} %win_hbm.1, ...), custom_call_target="tpu_custom_call" | custom-call | tf_op jit(solution)/shard_map/pair_attention_backward/pallas_call | solution.py:662
  70.8 2.5 %hand_over.1 = (bf16[16,64,1024]{2,1,0:T(8,128)(2,1)}, bf16[1,32,512]{2,1,0:T(8,128)(2,1)}, bf16[1,32,1024]{2,1,0:T(8,128)(2,1)}, bf16[1,32,1024]{2,1,0:T(8,128)(2,1)}) custom-call(bf16[16,64,1024]{2,1,0:T(8,128)(2,1)} %get-tuple-element.8.gp_in, bf16[1,32,512]{2,1,0:T(8,128)(2,1)} %get-tuple-element.9.gq_in, bf16[1,32,1024]{2,1,0:T(8,128)(2,1)} %get-tuple-element.10.gk_in, ...), custom_call_target="tpu_custom_call" | custom-call | tf_op jit(solution)/shard_map/hand_over/pallas_call | solution.py:729

commit v4 on v3

--- a/solution.py
+++ b/solution.py
@@ -52,7 +52,7 @@
     q_v, out_v, dout_v, norm_v,
     gp_v, gq_v, gkv_v,
     slope_v, stat_v, kv_v, bias_out, bias_in, ds_all, ds_in, probs_v, probs_f,
-    qstage, qrecv, qblk_v, doblk_v, norm_b, delta_b, dkv_v,
+    qstage, qrecv, qblk_v, doblk_v, qt_v, dot_v, norm_b, delta_b, dkv_v,
     rsp_send, rsp_recv, rsm_send, rsm_recv,
     dq_send, dq_recv, dq_peers, w1_v, w2_v, wmix_v, tab_v,
     in_sem, x_sem, kv_sem, gp_sem, o_sem,
@@ -191,14 +191,22 @@
 
             @pl.when(source // 8 == core)
             def _():
-                onward = [ag_copy(half, source % 8, way, hop) for hop in ((1,) if way == 1 and hops == 6 else (2, 1))]
+                two, one = (ag_copy(half, source % 8, way, hop) for hop in (2, 1))
+                needed = source % 2 == way if hops == 6 else source >= 0
                 if ending:
-                    for copy in onward:
-                        copy.wait_send()
+                    one.wait_send()
+
+                    @pl.when(needed)
+                    def _():
+                        two.wait_send()
                 else:
-                    onward[0].wait_recv()
-                    for copy in onward:
-                        copy.start()
+                    one.wait_recv()
+
+                    @pl.when(needed)
+                    def _():
+                        two.start()
+
+                    one.start()
 
     def ag_finish(half):
         for way, hops in ((0, 1), (0, 3), (0, 5), (0, 7), (0, 8), (1, 1), (1, 3), (1, 5), (1, 7)):
@@ -321,6 +329,8 @@
     own_head = iota((512, 256), 0) % 8 == iota((512, 256), 1) // 32
     qblk_v[...] = jnp.where(own_head, dot(by_row, ones_where(lane == spot % 32)), 0.0).astype(BF16)
     doblk_v[...] = jnp.where(own_head, dot(by_row, ones_where(lane == 32 + spot % 32)), 0.0).astype(BF16)
+    qt_v[...] = qblk_v[...].T
+    dot_v[...] = doblk_v[...].T
     wide = iota((128, 128), 0)
     norm_b[...] = dot(by_row, ones_where(jnp.logical_and(wide >= 64, wide < 67)))
     delta_b[...] = dot(by_row, ones_where(jnp.logical_and(wide >= 67, wide < 70)))
@@ -343,7 +353,7 @@
         probs = jnp.where(live, jnp.exp(scores - shift), 0.0)
         probs_f[rows, :] = probs
         probs_v[rows, :] = probs.astype(BF16)
-    dkv_v[:, 32:64, :] = dot(doblk_v[...].T, probs_v[...]).reshape(8, 32, 1024)
+    dkv_v[:, 32:64, :] = dot(dot_v[...], probs_v[...]).reshape(8, 32, 1024)
 
     def rs_copy(way, far, half):
         hops = 2 if far == 8 or far % 2 == 0 else 1
@@ -361,28 +371,36 @@
     def rs_part(far, half, way):
         dest = rs_dest(way, far)
         send, recv = ((rsp_send, rsp_recv), (rsm_send, rsm_recv))[way]
-        last = 7 if way else 8
-
-        @pl.when(dest // 8 == core)
+        needed = dest // 8 == core
+        if far == 8:
+            needed = jnp.logical_and(needed, dest % 2 == way)
+
+        @pl.when(needed)
         def _():
             total = dkv_v[dest % 8, half * 32:half * 32 + 32, :]
             if far in (2, 4, 6):
                 for other in (far + 1, far + 2):
-                    if other <= last:
+                    if other < 8:
                         rs_copy(way, other, half).wait_recv()
                         total = total + recv[other - 1, half].astype(F32)
             send[far - 1, half] = total.astype(BF16)
+            if far == 6:
+                @pl.when(dest % 2 == way)
+                def _():
+                    rs_copy(way, 8, half).wait_recv()
+                    send[far - 1, half] = (total + recv[7, half].astype(F32)).astype(BF16)
+
             rs_copy(way, far, half).start()
 
     def rs_raw(half):
-        for far in (8, 7, 5, 3, 1):
+        for far in (8, 7):
             for way in range(2):
-                if not (way == 1 and far == 8):
-                    rs_part(far, half, way)
+                rs_part(far, half, way)
 
     def rs_sum(far, half):
-        for way in range(2):
-            rs_part(far, half, way)
+        for at in (far, far - 1):
+            for way in range(2):
+                rs_part(at, half, way)
 
     rs_raw(1)
     ag_finish(1)
@@ -412,10 +430,12 @@
         ds_all[part] = dscores
         if not step:
             ds_in[part] = dscores
-    for piece in range(4):
-        for step in (1, 3, 2):
-            ds_copy(step, piece).start()
     ds_flat = ds_all[...].reshape(512, 1024)
+    dkv_v[:, 0:32, :] = dot(qt_v[...], ds_flat).reshape(8, 32, 1024)
+    rs_raw(0)
+    for step in (1, 3, 2):
+        ds_copy(step, 0).start()
+
     dq_full = lax.dot_general(ds_flat, keys, (((1,), (1,)), ((), ())), preferred_element_type=F32)
     dq_full = jnp.where(own_head, dq_full, 0.0)
     dq_fold = dq_full[:, 0:128] + dq_full[:, 128:256]
@@ -460,9 +480,9 @@
     def _():
         dq_recv[zpos] = dq_send[slot * 2 + core]
 
-    dkv_v[:, 0:32, :] = dot(qblk_v[...].T, ds_flat).reshape(8, 32, 1024)
-    rs_raw(0)
     rs_sum(6, 1)
+    for step in (1, 3, 2):
+        ds_copy(step, 1).start()
 
     def p2_copy(step):
         return pltpu.make_async_remote_copy(
@@ -520,12 +540,18 @@
                 ds_arrival(step, pair // 2).wait_recv()
 
         backward_pair(pair)
-        for at, (far, half) in ((1, (6, 0)), (2, (4, 1)), (4, (4, 0)), (6, (2, 1))):
+        for at in (0, 2):
+            @pl.when(pair == at)
+            def _():
+                for step in (1, 3, 2):
+                    ds_copy(step, at // 2 + 2).start()
+
+        for at, (far, half) in ((0, (6, 0)), (1, (4, 1)), (3, (4, 0)), (4, (2, 1))):
             @pl.when(pair == at)
             def _():
                 rs_sum(far, half)
 
-        @pl.when(pair == 5)
+        @pl.when(pair == 6)
         def _():
             phase_two()
 
@@ -614,9 +640,14 @@
             ds_copy(step, piece).wait_send()
 
     for half in range(2):
-        for way, last in ((0, 8), (1, 7)):
-            for far in range(1, last + 1):
-                @pl.when(rs_dest(way, far) // 8 == core)
+        for way in range(2):
+            for far in range(1, 9):
+                dest = rs_dest(way, far)
+                sent = dest // 8 == core
+                if far == 8:
+                    sent = jnp.logical_and(sent, dest % 2 == way)
+
+                @pl.when(sent)
                 def _():
                     rs_copy(way, far, half).wait_send()
 
@@ -698,13 +729,15 @@
             vmem((16, 32, 128), BF16),
             vmem((512, 256), BF16),
             vmem((512, 256), BF16),
+            vmem((256, 512), BF16),
+            vmem((256, 512), BF16),
             vmem((512, 128), F32),
             vmem((512, 128), F32),
             vmem((8, 64, 1024), F32),
             vmem((8, 2, 32, 1024), BF16),
             vmem((8, 2, 32, 1024), BF16),
-            vmem((7, 2, 32, 1024), BF16),
-            vmem((7, 2, 32, 1024), BF16),
+            vmem((8, 2, 32, 1024), BF16),
+            vmem((8, 2, 32, 1024), BF16),
             vmem((16, 8, 128), F32),
             vmem((16, 8, 128), F32),
             vmem((8, 128, 128), BF16),
@@ -714,7 +747,7 @@
             vmem((32, 32), BF16),
             dma((11,)), dma((8,)), dma((2,)), dma((8,)), dma((3,)),
             dma((2, 4, 8)), dma((2, 8)), dma((16,)), dma((16,)), dma((4,)), dma((4,)), dma((4, 4)), dma((4, 4)),
-            dma((8, 2)), dma((8, 2)), dma((7, 2)), dma((7, 2)), dma, dma,
+            dma((8, 2)), dma((8, 2)), dma((8, 2)), dma((8, 2)), dma, dma,
             dma((16,)), dma((16,)), dma((8,)), dma((8,)),
             pltpu.SemaphoreType.REGULAR, pltpu.SemaphoreType.REGULAR,
         ],

time: 74.3 us -> 72.5 us (0.976)
  Pallas kernels: 72.7 us -> 71.6 us
    pallas_call x1, Pallas kernels: 70.2 us -> 69.1 us  [per_device(): pl.pallas_call(kernel, out_shape=(jax.ShapeDtypeStruct((16, 64, 1024), BF...]
where the time goes in v4:
time: 72.5 us; the launch traced here: 72.3 us
  Pallas kernels  71.6 us (99%)
    pallas_call x1, Pallas kernels, per_device(): pl.pallas_call(kernel, out_shape=(jax.ShapeDtypeStruct((16, 64, 1024), BF...  69.1 us
    pallas_call x1, Pallas kernels, per_device(): pl.pallas_call(hand_over, out_shape=tuple((jax.ShapeDtypeStruct(member.sh...  2.54 us

profile of v4, /device:TPU:1, one launch (start us, length us, event | category | flops | bytes accessed | tf_op | source)
XLA Modules:
  0.0 72.3 jit_solution(6626991670639989147)
XLA Ops:
  0.6 69.1 %pair_attention_backward.1 = (bf16[16,64,1024]{2,1,0:T(8,128)(2,1)}, bf16[1,32,512]{2,1,0:T(8,128)(2,1)}, bf16[1,32,1024]{2,1,0:T(8,128)(2,1)}, bf16[1,32,1024]{2,1,0:T(8,128)(2,1)}) custom-call(bf16[16,64,1024]{2,1,0:T(8,128)(2,1)} %x_hbm.1, s32[16,1024]{1,0:T(8,128)} %bucket_hbm.1, f32[1,64]{1,0:T(1,128)} %bitcast.7, bf16[64,256]{1,0:T(8,128)(2,1)} %win_hbm.1, ...), custom_call_target="tpu_custom_call" | custom-call | tf_op jit(solution)/shard_map/pair_attention_backward/pallas_call | solution.py:693
  69.7 2.5 %hand_over.1 = (bf16[16,64,1024]{2,1,0:T(8,128)(2,1)}, bf16[1,32,512]{2,1,0:T(8,128)(2,1)}, bf16[1,32,1024]{2,1,0:T(8,128)(2,1)}, bf16[1,32,1024]{2,1,0:T(8,128)(2,1)}) custom-call(bf16[16,64,1024]{2,1,0:T(8,128)(2,1)} %get-tuple-element.8.gp_in, bf16[1,32,512]{2,1,0:T(8,128)(2,1)} %get-tuple-element.9.gq_in, bf16[1,32,1024]{2,1,0:T(8,128)(2,1)} %get-tuple-element.10.gk_in, ...), custom_call_target="tpu_custom_call" | custom-call | tf_op jit(solution)/shard_map/hand_over/pallas_call | solution.py:762
